TPU v7x, 512 devices: a whole 4x8x8 slice. The times are simulated.
512 devices in a mesh: dp: 16 (over y, x_lo), comp: 32 (over z, x_hi, core).
Axes of the slice: x: 4 (x_hi: 2, x_lo: 2; x = x_hi * 2 + x_lo), y: 8, z: 8, core: 2. Of those that a mesh axis runs over, the one named last changes fastest.
Arguments:
- descriptors: float32 [32768, 128], P(('dp', 'comp')), may hold values from -10 to 10
- means: float32 [128, 16384], P(None, 'comp'), may hold values from -0.8 to 0.8
- variances: float32 [128, 16384], P(None, 'comp'), may hold values from 0.25 to 2
- log_weights: float32 [16384], P('comp'), may hold values from -3 to 0
Outputs:
- new_means: float32 [128, 16384], P('dp', 'comp')
- new_variances: float32 [128, 16384], P('dp', 'comp')
- new_log_weights: float32 [16384], P('comp')
- mean_loglik: float32 [], replicated
All inputs are finite; a program needn't handle non-finite values.
Results may differ from a plain program's by a relative error of at most 0.0003.
Values sent between devices are 32-bit elements; how exact they have to be, the bound alone decides.
A program may use at most 64 MiB of HBM per device.

v0:
```python
import math

import jax
import jax.numpy as jnp
from jax import lax
from jax.sharding import PartitionSpec as P

LOG_TWO_PI = math.log(2.0 * math.pi)
PRIOR = 1.0


def matmul(left, right):
    return jnp.dot(left, right, precision=lax.Precision.HIGHEST, preferred_element_type=jnp.float32)


def local(descriptors, means, variances, log_weights):
    dims = means.shape[0]
    precision_mat = 1.0 / variances
    linear = means * precision_mat
    offset = (
        log_weights
        - 0.5 * jnp.sum(means * linear, 0)
        - 0.5 * jnp.sum(jnp.log(variances), 0)
        - 0.5 * dims * LOG_TWO_PI
    )
    local_rows = descriptors.shape[0]
    groups = lax.axis_size("comp")
    gathered_rows = local_rows * groups
    blocks = max(1, gathered_rows // 1024)
    block_size = gathered_rows // blocks
    comp_local = means.shape[1]
    gathered = lax.all_gather(descriptors, "comp", axis=0, tiled=True)
    counts = jnp.zeros((comp_local,), jnp.float32)
    first = jnp.zeros((dims, comp_local), jnp.float32)
    second = jnp.zeros((dims, comp_local), jnp.float32)
    loglik = jnp.zeros((), jnp.float32)
    for number in range(blocks):
        rows = gathered[number * block_size : (number + 1) * block_size]
        squares = rows * rows
        scores = -0.5 * matmul(squares, precision_mat) + matmul(rows, linear) + offset
        top = lax.pmax(jnp.max(scores, 1), "comp")
        total = lax.psum(jnp.sum(jnp.exp(scores - top[:, None]), 1), "comp")
        norm = top + jnp.log(total)
        resp = jnp.exp(scores - norm[:, None])
        counts = counts + jnp.sum(resp, 0)
        first = first + matmul(rows.T, resp)
        second = second + matmul(squares.T, resp)
        loglik = loglik + jnp.sum(norm)
    first_part, second_part = (
        lax.psum_scatter(first, "dp", scatter_dimension=0, tiled=True),
        lax.psum_scatter(second, "dp", scatter_dimension=0, tiled=True),
    )
    counts, loglik = lax.psum((counts, loglik), "dp")
    owned = first_part.shape[0]
    start = lax.axis_index("dp") * owned
    means_part = lax.dynamic_slice_in_dim(means, start, owned, 0)
    variances_part = lax.dynamic_slice_in_dim(variances, start, owned, 0)
    denom = counts + PRIOR
    new_means = (first_part + PRIOR * means_part) / denom
    scatter = second_part - 2.0 * means_part * first_part + means_part * means_part * counts
    new_variances = (scatter + PRIOR * variances_part) / denom
    total_rows = gathered_rows * lax.axis_size("dp")
    all_comps = comp_local * groups
    new_log_weights = jnp.log((counts + PRIOR) / (total_rows + all_comps * PRIOR))
    mean_loglik = loglik / (total_rows * dims)
    return (new_means, new_variances, new_log_weights, mean_loglik)


def solution(mesh):
    placed = (P(("dp", "comp"), None), P(None, "comp"), P(None, "comp"), P("comp"))
    return jax.shard_map(
        local,
        mesh=mesh,
        in_specs=placed,
        out_specs=(P("dp", "comp"), P("dp", "comp"), P("comp"), P()),
        check_vma=False,
    )
```

profile of v0, /device:TPU:4, one launch (start us, length us, event | category | flops | bytes accessed | tf_op | source)
XLA Modules:
  0.0 405.1 jit_solution(15663945424928719993)
XLA Ops:
  7.2 0.0 copy-start.3
  7.2 0.0 all-gather.2.cloned.1.call-start
  7.2 0.7 all-gather.2.cloned.1.call-update
  7.9 0.0 reduce-scatter.7.cloned.1.call-start
  8.0 0.7 constant_dynamic-slice_fusion
  8.7 0.8 copy.23
  9.5 0.9 copy.24
  10.4 1.1 multiply_reduce_fusion
  11.5 0.7 subtract_add_fusion
  12.2 85.8 %all-gather.2.cloned.1.call-done = f32[2048,128]{1,0:T(8,128)} async-done(((f32[64,128]{1,0:T(8,128)}), f32[2048,128]{1,0:T(8,128)}) %all-gather.2.cloned.1.call-update) | async-done | bytes 1048592 | tf_op jit(solution)/shard_map/all_gather | solution.py:32
  98.0 3.0 fusion.19
  101.1 0.0 copy-done.3
  101.1 0.0 copy-done.2
  101.1 0.0 copy-start.4
  101.1 1.8 fusion.16
  102.9 0.0 copy-done.4
  103.0 2.2 fusion.33
  105.1 3.5 fusion.34
  108.6 64.2 %all-reduce.1 = (f32[1024]{0:T(1024)S(1)}, f32[1024]{0:T(1024)S(1)}) all-reduce(f32[1024]{0:T(1024)S(1)} %get-tuple-element.28, f32[1024]{0:T(1024)S(1)} %get-tuple-element.30), channel_id=1, replica_groups=mesh['dp'=16,'comp'=32] {'comp'}, use_global_device_ids=true, to_apply=%region_3.0 | all-reduce | flops 2048 | bytes 16384 | tf_op jit(solution)/shard_map/pmax | solution.py:41
  172.9 1.9 exponential_reduce_fusion
  174.8 0.3 exponential_reduce_fusion.1
  175.1 66.2 %all-reduce = (f32[1024]{0:T(1024)S(1)}, f32[1024]{0:T(1024)S(1)}) all-reduce(f32[1024]{0:T(1024)S(1)} %exponential_reduce_fusion.1, f32[1024]{0:T(1024)S(1)} %exponential_reduce_fusion), channel_id=1, replica_groups=mesh['dp'=16,'comp'=32] {'comp'}, use_global_device_ids=true, to_apply=%region_5.0 | all-reduce | flops 2048 | bytes 16384 | tf_op jit(solution)/shard_map/psum | solution.py:42
  241.3 0.0 copy-start
  241.3 0.6 fusion.31
  241.9 1.9 fusion.4
  243.8 0.0 copy-done
  243.8 1.9 fusion.9
  245.7 0.9 copy.19
  246.6 0.0 reduce-scatter.7.cloned.1.call-update
  246.6 0.0 reduce-scatter.9.cloned.1.call-start
  246.6 0.0 copy-start.1
  246.6 2.5 fusion.2
  249.1 0.0 copy-done.1
  249.2 3.2 fusion.10
  252.4 0.0 reduce-scatter.9.cloned.1.call-update
  252.4 0.0 copy-start.5
  252.4 0.0 copy-start.6
  252.4 2.0 fusion.6
  255.7 0.4 fusion.3
  256.1 35.2 %all-reduce.2 = (f32[512]{0:T(512)S(1)}, f32[]{:T(128)}) all-reduce(f32[512]{0:T(512)S(1)} %add.82, f32[]{:T(128)S(6)} %add.87), channel_id=1, replica_groups=mesh['dp'=16,'comp'=32] {'dp'}, use_global_device_ids=true, to_apply=%region_13.0 | all-reduce | flops 513 | bytes 4104 | tf_op jit(solution)/shard_map/psum | solution.py:53
  292.0 0.6 multiply_log_fusion
  292.5 28.4 %reduce-scatter.7.cloned.1.call-done = f32[8,512]{1,0:T(8,128)} async-done(((f32[128,512]{1,0:T(8,128)}), f32[8,512]{1,0:T(8,128)}) %reduce-scatter.7.cloned.1.call-update) | async-done | bytes 16400
  320.9 0.8 copy.20
  321.8 73.2 %reduce-scatter.9.cloned.1.call-done = f32[8,512]{1,0:T(8,128)} async-done(((f32[128,512]{1,0:T(8,128)}), f32[8,512]{1,0:T(8,128)}) %reduce-scatter.9.cloned.1.call-update) | async-done | bytes 16400
  395.0 0.8 copy.22
  395.8 0.2 add_divide_fusion
  396.1 0.7 copy.17
  396.8 0.7 copy.18
  (4 shorter events, 0.0 us)
Async XLA Ops:
  7.2 93.9 %copy-start.3 = (f32[128,512]{1,0:T(8,128)S(1)}, f32[128,512]{1,0:T(8,128)}, u32[]{:S(2)}) copy-start(f32[128,512]{1,0:T(8,128)} %param.6) | copy-start | bytes 786436
  7.2 90.8 %all-gather.2.cloned.1.call-start = ((), (), s32[]{:S(2)}) async-start(), calls=%async_computation.2 | async-start | bytes 1081344 | tf_op jit(solution)/shard_map/all_gather | solution.py:32
  7.9 313.0 %reduce-scatter.7.cloned.1.call-start = ((), (), s32[]{:S(2)}) async-start(), calls=%async_computation.3 | async-start | bytes 278528
  98.0 3.0 copy-start.2
  101.1 1.9 copy-start.4
  241.3 2.5 copy-start
  246.6 148.4 %reduce-scatter.9.cloned.1.call-start = ((), (), s32[]{:S(2)}) async-start(), calls=%async_computation.4 | async-start | bytes 278528
  246.6 2.5 copy-start.1
  252.4 143.4 %copy-start.5 = (f32[8,512]{0,1:T(8,128)S(1)}, f32[8,512]{0,1:T(8,128)}, u32[]{:S(2)}) copy-start(f32[8,512]{0,1:T(8,128)} %copy.23) | copy-start | bytes 49156
  252.4 143.4 %copy-start.6 = (f32[8,512]{0,1:T(8,128)S(1)}, f32[8,512]{0,1:T(8,128)}, u32[]{:S(2)}) copy-start(f32[8,512]{0,1:T(8,128)} %copy.24) | copy-start | bytes 49156
Sparse Core Ops, SparseCore 0:
  11.4 86.5 all-gather.1
  246.7 74.1 reduce-scatter.6
  324.0 70.9 reduce-scatter.8
where the time goes:
time: 406 us; the launch traced here: 405 us
  waiting for transfers between devices  188 us (46%)
  blocking collectives  166 us (41%)
  matrix products  20 us (5%)
  between operations  17 us (4%)
  other arithmetic  7.85 us (2%)
  local copies, waits for them, and re-layouts  6.41 us (2%)
    unnamed x5, waiting for transfers between devices  102 us
    all_gather x1, waiting for transfers between devices, local(): gathered = lax.all_gather(descriptors, 'comp', axis=0, tiled=True)  85.8 us
    psum x1, blocking collectives, local(): total = lax.psum(jnp.sum(jnp.exp(scores - top[:, None]), 1), 'comp')  66.2 us
    pmax x1, blocking collectives, local(): top = lax.pmax(jnp.max(scores, 1), 'comp')  64.2 us
    psum x1, blocking collectives, local(): counts, loglik = lax.psum((counts, loglik), 'dp')  35.2 us
    dot_general x8, matrix products, matmul(): jnp.dot(left, right, precision=lax.Precision.HIGHEST, preferred_element_t...  20 us
  transfers between devices with their start and end apart: 3, of which 3 were waited for; matrix products, arithmetic and copies ran while one was open for 3% of the time, Pallas kernels for 0%

commit v1 on v0

v1 whole, which is shorter than its diff:
```python
import math

import jax
import jax.numpy as jnp
from jax import lax
from jax.experimental import pallas as pl
from jax.experimental.pallas import tpu as pltpu
from jax.sharding import PartitionSpec as P

LOG_TWO_PI = math.log(2.0 * math.pi)
PRIOR = 1.0
MESH = pl.DeviceIdType.MESH
D = 128
ROWS = 64
NZ, NY = 8, 8
COMPS = 512
BLOCK = 4 * ROWS
CHUNK = 128
CHUNKS = COMPS // CHUNK
TOTAL_ROWS = 32768
TOTAL_COMPS = 16384
F32, BF16 = jnp.float32, jnp.bfloat16


def split(a):
    hi = a.astype(BF16)
    return hi, (a - hi.astype(F32)).astype(BF16)


def dot_nt(a, b):
    return lax.dot_general(a, b, (((1,), (1,)), ((), ())), preferred_element_type=F32)


def dot_nn(a, b):
    return lax.dot_general(a, b, (((1,), (0,)), ((), ())), preferred_element_type=F32)


def kernel(
    x_hbm, means_hbm, var_hbm, lw_hbm,
    nm_ref, nv_ref, nlw_ref, ll_ref,
    means, var, lw, xg, p_hi, p_lo, off, f_hi, f_lo, e_buf, lse, lmax, lse_in, part, part_in,
    p1, p1_in, p2, p2_in, cnt, cnt_in, cnt2, cnt2_in,
    in_sem, gz_s, gx_s, gc_s, g_r, l_s, l_r, lc_s, lc_r, p1_s, p1_r, p2_s, p2_r, c1_s, c1_r, c2_s, c2_r,
):
    d = lax.axis_index("dp")
    c = lax.axis_index("comp")
    y, xlo = d // 2, d % 2
    core = c % 2
    xhi = (c // 2) % 2
    z = c // 4

    def at(dz, dx, dc):
        nz = (z + dz) % NZ
        nx = 1 - xhi if dx else xhi
        nc = 1 - core if dc else core
        return (d, nz * 4 + nx * 2 + nc)

    def y_peer(dy):
        return (((y + dy) % NY) * 2 + xlo, c)

    xlo_peer = (y * 2 + 1 - xlo, c)

    local_in = [
        pltpu.make_async_copy(means_hbm, means, in_sem.at[0]),
        pltpu.make_async_copy(var_hbm, var, in_sem.at[1]),
        pltpu.make_async_copy(lw_hbm, lw, in_sem.at[2]),
        pltpu.make_async_copy(x_hbm, xg.at[0, pl.ds(0, ROWS)], in_sem.at[3]),
    ]
    for copy in local_in:
        copy.start()

    barrier = pltpu.get_barrier_semaphore()
    peers = [at(dz, 0, 0) for dz in range(1, NZ)] + [at(0, 1, 0), at(0, 0, 1), xlo_peer]
    peers += [y_peer(dy) for dy in range(1, NY)]
    for peer in peers:
        pl.semaphore_signal(barrier, inc=1, device_id=peer, device_id_type=MESH)
    for copy in local_in:
        copy.wait()
    pl.semaphore_wait(barrier, len(peers))

    def block(rz, sub):
        return xg.at[rz, pl.ds(ROWS * sub, ROWS)]

    def remote(src, dst, send, recv, peer):
        return pltpu.make_async_remote_copy(
            src_ref=src, dst_ref=dst, send_sem=send, recv_sem=recv, device_id=peer, device_id_type=MESH
        )

    def z_copy(dz):
        rz = (NZ - dz) % NZ
        return remote(block(0, 0), block(rz, 0), gz_s.at[dz], g_r.at[rz, 0], at(dz, 0, 0))

    def z_arrival(rz):
        return remote(block(0, 0), block(rz, 0), gz_s.at[0], g_r.at[rz, 0], at(0, 0, 1))

    def x_copy(rz):
        return remote(block(rz, 0), block(rz, 2), gx_s.at[rz], g_r.at[rz, 2], at(0, 1, 0))

    def core_copy(rz, sub):
        return remote(
            block(rz, sub), block(rz, sub + 1), gc_s.at[rz, sub], g_r.at[rz, sub + 1], at(0, 0, 1)
        )

    for dz in (4, 3, 5, 2, 6, 1, 7):
        z_copy(dz).start()
    x_copy(0).start()
    core_copy(0, 0).start()

    prec = 1.0 / var[...]
    lin = means[...] * prec
    offset = (
        lw[...]
        - 0.5 * jnp.sum(means[...] * lin, 0, keepdims=True)
        - 0.5 * jnp.sum(jnp.log(var[...]), 0, keepdims=True)
        - 0.5 * D * LOG_TWO_PI
    )
    off[...] = jnp.broadcast_to(offset, (D, COMPS)).T
    for part_number, a in enumerate((-0.5 * prec, lin)):
        hi, lo = split(a.T)
        p_hi[:, pl.ds(D * part_number, D)] = hi
        p_lo[:, pl.ds(D * part_number, D)] = lo

    def e_step(rz):
        rows = xg[rz]
        sq_hi, sq_lo = split(rows * rows)
        x_hi, x_lo = split(rows)
        f_hi[rz, :, pl.ds(0, D)] = sq_hi
        f_hi[rz, :, pl.ds(D, D)] = x_hi
        f_lo[rz, :, pl.ds(0, D)] = sq_lo
        f_lo[rz, :, pl.ds(D, D)] = x_lo
        fh, fl = f_hi[rz], f_lo[rz]
        s = dot_nt(p_hi[...], fh) + dot_nt(p_lo[...], fh) + dot_nt(p_hi[...], fl)
        s = s + jnp.concatenate([off[...], off[...]], 1)
        top = jnp.max(s, 0, keepdims=True)
        e = jnp.exp(s - top)
        e_buf[rz] = e
        total = jnp.sum(e, 0, keepdims=True)
        lmax[pl.ds(rz, 1), :] = top
        lse[pl.ds(rz, 1), :] = top + jnp.log(total)

    def order(i):
        return ((i % 2) * (i + 1) // 2 + (1 - i % 2) * (NZ - i // 2)) % NZ

    def forward_z(rz):
        z_arrival(rz).wait_recv()
        x_copy(rz).start()
        core_copy(rz, 0).start()

    def forward_x(rz):
        x_copy(rz).wait_recv()
        core_copy(rz, 2).start()

    def arrived(rz):
        core_copy(rz, 0).wait_recv()
        core_copy(rz, 2).wait_recv()

    forward_z(order(1))
    forward_x(order(0))

    def gather_step(i, carry):
        @pl.when(i < NZ - 1)
        def _():
            forward_z(order(i + 1))

        forward_x(order(i))
        before = order(i - 1)
        arrived(before)
        e_step(before)
        return carry

    lax.fori_loop(1, NZ, gather_step, 0)
    arrived(order(NZ - 1))
    e_step(order(NZ - 1))

    def lse_copy(dz, dx):
        slot = 2 * ((NZ - dz) % NZ) + dx
        return remote(lse, lse_in.at[slot], l_s.at[2 * dz + dx], l_r.at[slot], at(dz, dx, 0))

    offsets = [(dz, dx) for dz in (4, 3, 5, 2, 6, 1, 7, 0) for dx in (1, 0) if (dz, dx) != (0, 0)]
    for dz, dx in offsets:
        lse_copy(dz, dx).start()
    for dz, dx in offsets:
        lse_copy(dz, dx).wait_recv()
    terms = [lse[...]]
    for dz, dx in offsets:
        rz = (NZ - dz) % NZ
        term = lse_in[2 * rz + dx]
        if rz:
            term = pltpu.roll(term, rz, 0)
        if dx:
            term = pltpu.roll(term, 2 * ROWS, 1)
        terms.append(term)
    top = terms[0]
    for term in terms[1:]:
        top = jnp.maximum(top, term)
    total = jnp.exp(terms[0] - top)
    for term in terms[1:]:
        total = total + jnp.exp(term - top)
    mine = top + jnp.log(total)
    part[...] = mine
    core_part = remote(part, part_in, lc_s, lc_r, at(0, 0, 1))
    core_part.start()
    core_part.wait_recv()
    other = part_in[...]
    other = jnp.concatenate(
        [pltpu.roll(other[:, : 2 * ROWS], ROWS, 1), pltpu.roll(other[:, 2 * ROWS :], ROWS, 1)], 1
    )
    top = jnp.maximum(mine, other)
    norm = top + jnp.log(jnp.exp(mine - top) + jnp.exp(other - top))
    lmax[...] = jnp.exp(lmax[...] - norm)
    loglik = jnp.sum(jnp.sum(norm, 0, keepdims=True), 1, keepdims=True)
    cnt[pl.ds(4, 4), :] = jnp.broadcast_to(loglik, (4, CHUNK))

    def p1_copy(ch):
        return remote(p1.at[ch, 1 - xlo], p1_in.at[ch], p1_s.at[ch], p1_r.at[ch], xlo_peer)

    def p2_copy(ch, dy):
        slot = (NY - dy) % NY
        return remote(
            p2.at[ch, (y + dy) % NY], p2_in.at[ch, slot], p2_s.at[ch, dy], p2_r.at[ch, slot], y_peer(dy)
        )

    def moments(ch):
        acc = jnp.zeros((CHUNK, 2 * D), F32)
        number = jnp.zeros((CHUNK, D), F32)
        comps = pl.ds(pl.multiple_of(ch * CHUNK, CHUNK), CHUNK)
        for rz in range(NZ):
            r = e_buf[rz, comps, :] * lmax[pl.ds(rz, 1), :]
            number = number + r[:, :D] + r[:, D:]
            hi, lo = split(r)
            acc = acc + dot_nn(hi, f_hi[rz]) + dot_nn(lo, f_hi[rz]) + dot_nn(hi, f_lo[rz])
        cnt[pl.ds(ch, 1), :] = jnp.sum(number.T, 0, keepdims=True)
        sq, fi = acc[:, :D].T, acc[:, D:].T
        for half in range(2):
            for ny in range(NY):
                at_row = 16 * ny + 8 * half
                p1[ch, half, ny, pl.ds(0, 8), :] = sq[at_row : at_row + 8]
                p1[ch, half, ny, pl.ds(8, 8), :] = fi[at_row : at_row + 8]
        p1_copy(ch).start()

    def pass_on(ch):
        p1_copy(ch).wait_recv()
        p2[ch] = p1[ch, xlo] + p1_in[ch]
        for dy in (4, 3, 5, 2, 6, 1, 7):
            p2_copy(ch, dy).start()

    moments(0)

    def moment_step(ch, carry):
        moments(ch)
        pass_on(ch - 1)
        return carry

    lax.fori_loop(1, CHUNKS, moment_step, 0)
    c1 = remote(cnt, cnt_in, c1_s, c1_r, xlo_peer)
    c1.start()
    pass_on(CHUNKS - 1)
    c1.wait_recv()
    cnt2[...] = cnt[...] + cnt_in[...]

    def c2_copy(dy):
        slot = (NY - dy) % NY
        return remote(cnt2, cnt2_in.at[slot], c2_s.at[dy], c2_r.at[slot], y_peer(dy))

    for dy in range(1, NY):
        c2_copy(dy).start()
    sums = [p2[ch, y] for ch in range(CHUNKS)]
    for dy in range(1, NY):
        for ch in range(CHUNKS):
            p2_copy(ch, dy).wait_recv()
    for dy in range(1, NY):
        c2_copy(dy).wait_recv()
    totals = cnt2[...]
    for dy in range(1, NY):
        totals = totals + cnt2_in[dy]
        sums = [sums[ch] + p2_in[ch, dy] for ch in range(CHUNKS)]
    own = pl.ds(pl.multiple_of(d * 8, 8), 8)
    for ch in range(CHUNKS):
        lanes = pl.ds(ch * CHUNK, CHUNK)
        counts = totals[ch : ch + 1, :]
        denom = counts + PRIOR
        second, first = sums[ch][:8], sums[ch][8:]
        m, v = means[own, lanes], var[own, lanes]
        nm_ref[:, lanes] = (first + PRIOR * m) / denom
        scatter = second - 2.0 * m * first + m * m * counts
        nv_ref[:, lanes] = (scatter + PRIOR * v) / denom
        nlw_ref[:, lanes] = jnp.log(denom / (TOTAL_ROWS + TOTAL_COMPS * PRIOR))
    ll_ref[...] = totals[4:5, :1] / (TOTAL_ROWS * D)

    for dz in range(1, NZ):
        z_copy(dz).wait_send()
    for rz in range(NZ):
        x_copy(rz).wait_send()
        core_copy(rz, 0).wait_send()
        core_copy(rz, 2).wait_send()
    for dz, dx in offsets:
        lse_copy(dz, dx).wait_send()
    core_part.wait_send()
    c1.wait_send()
    for ch in range(CHUNKS):
        p1_copy(ch).wait_send()
        for dy in range(1, NY):
            p2_copy(ch, dy).wait_send()
    for dy in range(1, NY):
        c2_copy(dy).wait_send()


def local(descriptors, means, variances, log_weights):
    sem = pltpu.SemaphoreType.DMA
    vmem = pltpu.VMEM
    nm, nv, nlw, ll = pl.pallas_call(
        kernel,
        out_shape=(
            jax.ShapeDtypeStruct((8, COMPS), F32),
            jax.ShapeDtypeStruct((8, COMPS), F32),
            jax.ShapeDtypeStruct((1, COMPS), F32),
            jax.ShapeDtypeStruct((1, 1), F32),
        ),
        in_specs=[pl.BlockSpec(memory_space=pl.ANY)] * 4,
        out_specs=(pl.BlockSpec(memory_space=pltpu.VMEM),) * 4,
        scratch_shapes=[
            vmem((D, COMPS), F32),
            vmem((D, COMPS), F32),
            vmem((1, COMPS), F32),
            vmem((NZ, BLOCK, D), F32),
            vmem((COMPS, 2 * D), BF16),
            vmem((COMPS, 2 * D), BF16),
            vmem((COMPS, D), F32),
            vmem((NZ, BLOCK, 2 * D), BF16),
            vmem((NZ, BLOCK, 2 * D), BF16),
            vmem((NZ, COMPS, BLOCK), F32),
            vmem((NZ, BLOCK), F32),
            vmem((NZ, BLOCK), F32),
            vmem((2 * NZ, NZ, BLOCK), F32),
            vmem((NZ, BLOCK), F32),
            vmem((NZ, BLOCK), F32),
            vmem((CHUNKS, 2, NY, 16, CHUNK), F32),
            vmem((CHUNKS, NY, 16, CHUNK), F32),
            vmem((CHUNKS, NY, 16, CHUNK), F32),
            vmem((CHUNKS, NY, 16, CHUNK), F32),
            vmem((8, CHUNK), F32),
            vmem((8, CHUNK), F32),
            vmem((8, CHUNK), F32),
            vmem((NY, 8, CHUNK), F32),
            sem((4,)),
            sem((NZ,)),
            sem((NZ,)),
            sem((NZ, 4)),
            sem((NZ, 4)),
            sem((2 * NZ,)),
            sem((2 * NZ,)),
            sem,
            sem,
            sem((CHUNKS,)),
            sem((CHUNKS,)),
            sem((CHUNKS, NY)),
            sem((CHUNKS, NY)),
            sem,
            sem,
            sem((NY,)),
            sem((NY,)),
        ],
        compiler_params=pltpu.CompilerParams(
            collective_id=0, has_side_effects=True, vmem_limit_bytes=40 * 2**20
        ),
        name="em_step",
    )(descriptors, means, variances, log_weights.reshape(1, COMPS))
    return nm, nv, nlw.reshape(COMPS), ll.reshape(())


def solution(mesh):
    placed = (P(("dp", "comp"), None), P(None, "comp"), P(None, "comp"), P("comp"))
    return jax.shard_map(
        local,
        mesh=mesh,
        in_specs=placed,
        out_specs=(P("dp", "comp"), P("dp", "comp"), P("comp"), P()),
        check_vma=False,
    )
```

time: 406 us -> 73.7 us (0.18)
  the two profiles are of different devices: /device:TPU:4 before, /device:TPU:1 now
where the time goes in v1:
time: 73.7 us; the launch traced here: 73.4 us
  Pallas kernels  65.9 us (89%)
  local copies, waits for them, and re-layouts  5.12 us (7%)
  between operations  2.4 us (3%)
    pallas_call x1, Pallas kernels, local(): pl.pallas_call(kernel, out_shape=(jax.ShapeDtypeStruct((8, COMPS), F32),...  65.9 us
    unnamed x11, local copies, waits for them, and re-layouts  5.12 us

profile of v1, /device:TPU:1, one launch (start us, length us, event | category | flops | bytes accessed | tf_op | source)
XLA Modules:
  0.0 73.4 jit_solution(3392413319489904413)
XLA Ops:
  0.6 0.0 copy-start
  0.6 0.9 %copy-done = f32[128,512]{1,0:T(8,128)S(1)} copy-done((f32[128,512]{1,0:T(8,128)S(1)}, f32[128,512]{1,0:T(8,128)}, u32[]{:S(2)}) %copy-start) | copy-done | bytes 262168
  1.6 0.0 copy-start.1
  1.6 0.9 %copy-done.1 = f32[128,512]{1,0:T(8,128)S(1)} copy-done((f32[128,512]{1,0:T(8,128)S(1)}, f32[128,512]{1,0:T(8,128)}, u32[]{:S(2)}) %copy-start.1) | copy-done | bytes 262168
  2.5 0.0 copy-start.2
  2.5 0.8 %copy-done.2 = f32[64,128]{1,0:T(8,128)S(1)} copy-done((f32[64,128]{1,0:T(8,128)S(1)}, f32[64,128]{1,0:T(8,128)}, u32[]{:S(2)}) %copy-start.2) | copy-done | bytes 32792
  3.3 0.0 copy-start.3
  3.3 0.7 copy-done.3
  4.0 65.9 %em_step.1 = (f32[8,512]{1,0:T(8,128)S(1)}, f32[8,512]{1,0:T(8,128)S(1)}, f32[1,512]{1,0:T(1,128)S(1)}, f32[1,1]{1,0:T(1,128)}) custom-call(f32[64,128]{1,0:T(8,128)S(1)} %copy-done.2, f32[128,512]{1,0:T(8,128)S(1)} %copy-done, f32[128,512]{1,0:T(8,128)S(1)} %copy-done.1, f32[1,512]{1,0:T(1,128)S(1)} %bitcast.3), custom_call_target="tpu_custom_call" | custom-call | tf_op jit(solution)/shard_map/em_step/pallas_call | solution.py:311
  69.8 0.6 copy.12
  70.4 0.6 copy.13
  71.1 0.6 copy.14
Async XLA Ops:
  0.6 1.0 %copy-start = (f32[128,512]{1,0:T(8,128)S(1)}, f32[128,512]{1,0:T(8,128)}, u32[]{:S(2)}) copy-start(f32[128,512]{1,0:T(8,128)} %means_hbm.1) | copy-start | bytes 786436
  1.6 0.9 %copy-start.1 = (f32[128,512]{1,0:T(8,128)S(1)}, f32[128,512]{1,0:T(8,128)}, u32[]{:S(2)}) copy-start(f32[128,512]{1,0:T(8,128)} %var_hbm.1) | copy-start | bytes 786436
  2.5 0.8 %copy-start.2 = (f32[64,128]{1,0:T(8,128)S(1)}, f32[64,128]{1,0:T(8,128)}, u32[]{:S(2)}) copy-start(f32[64,128]{1,0:T(8,128)} %x_hbm.1) | copy-start | bytes 98308
  3.3 0.7 copy-start.3

commit v2 on v1

--- a/solution.py
+++ b/solution.py
@@ -14,7 +14,13 @@
 ROWS = 64
 NZ, NY = 8, 8
 COMPS = 512
-BLOCK = 4 * ROWS
+PAIR = 2 * ROWS
+BLOCK = 2 * PAIR
+UNITS = (
+    ((0, 0), (1, 0)), ((0, 1), (0, 7)), ((0, 2), (0, 6)), ((1, 1), (1, 7)),
+    ((0, 3), (0, 5)), ((1, 2), (1, 6)), ((0, 4), (1, 4)), ((1, 3), (1, 5)),
+)
+SENDS = 15
 CHUNK = 128
 CHUNKS = COMPS // CHUNK
 TOTAL_ROWS = 32768
@@ -40,7 +46,7 @@
     nm_ref, nv_ref, nlw_ref, ll_ref,
     means, var, lw, xg, p_hi, p_lo, off, f_hi, f_lo, e_buf, lse, lmax, lse_in, part, part_in,
     p1, p1_in, p2, p2_in, cnt, cnt_in, cnt2, cnt2_in,
-    in_sem, gz_s, gx_s, gc_s, g_r, l_s, l_r, lc_s, lc_r, p1_s, p1_r, p2_s, p2_r, c1_s, c1_r, c2_s, c2_r,
+    in_sem, g_s, g_r, gc_s, gc_r, l_s, l_r, lc_s, lc_r, p1_s, p1_r, p2_s, p2_r, c1_s, c1_r, c2_s, c2_r,
 ):
     d = lax.axis_index("dp")
     c = lax.axis_index("comp")
@@ -64,13 +70,13 @@
         pltpu.make_async_copy(means_hbm, means, in_sem.at[0]),
         pltpu.make_async_copy(var_hbm, var, in_sem.at[1]),
         pltpu.make_async_copy(lw_hbm, lw, in_sem.at[2]),
-        pltpu.make_async_copy(x_hbm, xg.at[0, pl.ds(0, ROWS)], in_sem.at[3]),
+        pltpu.make_async_copy(x_hbm, xg.at[0, 0, pl.ds(0, ROWS)], in_sem.at[3]),
     ]
     for copy in local_in:
         copy.start()
 
     barrier = pltpu.get_barrier_semaphore()
-    peers = [at(dz, 0, 0) for dz in range(1, NZ)] + [at(0, 1, 0), at(0, 0, 1), xlo_peer]
+    peers = [at(dz, dx, 0) for dz in range(NZ) for dx in range(2) if dz or dx] + [at(0, 0, 1), xlo_peer]
     peers += [y_peer(dy) for dy in range(1, NY)]
     for peer in peers:
         pl.semaphore_signal(barrier, inc=1, device_id=peer, device_id_type=MESH)
@@ -78,32 +84,35 @@
         copy.wait()
     pl.semaphore_wait(barrier, len(peers))
 
-    def block(rz, sub):
-        return xg.at[rz, pl.ds(ROWS * sub, ROWS)]
+    def block(rx, rz, rc):
+        return xg.at[rx, rz, pl.ds(ROWS * rc, ROWS)]
 
     def remote(src, dst, send, recv, peer):
         return pltpu.make_async_remote_copy(
             src_ref=src, dst_ref=dst, send_sem=send, recv_sem=recv, device_id=peer, device_id_type=MESH
         )
 
-    def z_copy(dz):
-        rz = (NZ - dz) % NZ
-        return remote(block(0, 0), block(rz, 0), gz_s.at[dz], g_r.at[rz, 0], at(dz, 0, 0))
-
-    def z_arrival(rz):
-        return remote(block(0, 0), block(rz, 0), gz_s.at[0], g_r.at[rz, 0], at(0, 0, 1))
-
-    def x_copy(rz):
-        return remote(block(rz, 0), block(rz, 2), gx_s.at[rz], g_r.at[rz, 2], at(0, 1, 0))
-
-    def core_copy(rz, sub):
-        return remote(
-            block(rz, sub), block(rz, sub + 1), gc_s.at[rz, sub], g_r.at[rz, sub + 1], at(0, 0, 1)
+    started = []
+
+    def send(rx, rz, dz, dx):
+        number = len(started)
+        to_x, to_z = 1 - rx if dx else rx, (rz - dz) % NZ
+        copy = remote(
+            block(rx, rz, 0), block(to_x, to_z, 0), g_s.at[number], g_r.at[to_x, to_z], at(dz, dx, 0)
         )
-
-    for dz in (4, 3, 5, 2, 6, 1, 7):
-        z_copy(dz).start()
-    x_copy(0).start()
+        copy.start()
+        started.append(copy)
+
+    def core_copy(rx, rz):
+        return remote(block(rx, rz, 0), block(rx, rz, 1), gc_s.at[rx, rz], gc_r.at[rx, rz], at(0, 0, 1))
+
+    def arrival(rx, rz):
+        remote(block(rx, rz, 0), block(rx, rz, 0), g_s.at[0], g_r.at[rx, rz], at(0, 1, 0)).wait_recv()
+        core_copy(rx, rz).start()
+
+    for dz in (2, 6, 1, 7):
+        send(0, 0, dz, 0)
+    send(0, 0, 0, 1)
     core_copy(0, 0).start()
 
     prec = 1.0 / var[...]
@@ -120,57 +129,54 @@
         p_hi[:, pl.ds(D * part_number, D)] = hi
         p_lo[:, pl.ds(D * part_number, D)] = lo
 
-    def e_step(rz):
-        rows = xg[rz]
+    def e_step(u):
+        (ax, az), (bx, bz) = UNITS[u]
+        for rx, rz in UNITS[u]:
+            core_copy(rx, rz).wait_recv()
+        rows = jnp.concatenate([xg[ax, az], xg[bx, bz]], 0)
         sq_hi, sq_lo = split(rows * rows)
         x_hi, x_lo = split(rows)
-        f_hi[rz, :, pl.ds(0, D)] = sq_hi
-        f_hi[rz, :, pl.ds(D, D)] = x_hi
-        f_lo[rz, :, pl.ds(0, D)] = sq_lo
-        f_lo[rz, :, pl.ds(D, D)] = x_lo
-        fh, fl = f_hi[rz], f_lo[rz]
+        f_hi[u, :, pl.ds(0, D)] = sq_hi
+        f_hi[u, :, pl.ds(D, D)] = x_hi
+        f_lo[u, :, pl.ds(0, D)] = sq_lo
+        f_lo[u, :, pl.ds(D, D)] = x_lo
+        fh, fl = f_hi[u], f_lo[u]
         s = dot_nt(p_hi[...], fh) + dot_nt(p_lo[...], fh) + dot_nt(p_hi[...], fl)
         s = s + jnp.concatenate([off[...], off[...]], 1)
         top = jnp.max(s, 0, keepdims=True)
         e = jnp.exp(s - top)
-        e_buf[rz] = e
-        total = jnp.sum(e, 0, keepdims=True)
-        lmax[pl.ds(rz, 1), :] = top
-        lse[pl.ds(rz, 1), :] = top + jnp.log(total)
-
-    def order(i):
-        return ((i % 2) * (i + 1) // 2 + (1 - i % 2) * (NZ - i // 2)) % NZ
-
-    def forward_z(rz):
-        z_arrival(rz).wait_recv()
-        x_copy(rz).start()
-        core_copy(rz, 0).start()
-
-    def forward_x(rz):
-        x_copy(rz).wait_recv()
-        core_copy(rz, 2).start()
-
-    def arrived(rz):
-        core_copy(rz, 0).wait_recv()
-        core_copy(rz, 2).wait_recv()
-
-    forward_z(order(1))
-    forward_x(order(0))
-
-    def gather_step(i, carry):
-        @pl.when(i < NZ - 1)
-        def _():
-            forward_z(order(i + 1))
-
-        forward_x(order(i))
-        before = order(i - 1)
-        arrived(before)
-        e_step(before)
-        return carry
-
-    lax.fori_loop(1, NZ, gather_step, 0)
-    arrived(order(NZ - 1))
-    e_step(order(NZ - 1))
+        e_buf[u] = e
+        total = top + jnp.log(jnp.sum(e, 0, keepdims=True))
+        for half, (rx, rz) in enumerate(UNITS[u]):
+            lanes = slice(half * PAIR, (half + 1) * PAIR)
+            lmax[rx, pl.ds(rz, 1), :] = top[:, lanes]
+            lse[rx, pl.ds(rz, 1), :] = total[:, lanes]
+
+    side = 1 - 2 * core
+    far = (NZ - 2 * side) % NZ
+    arrival(0, 6)
+    arrival(0, 2)
+    send(0, far, 2 * side, 1)
+    send(0, far, 2 * side, 0)
+    for dx in (1, 0):
+        send(0, 6, 1, dx)
+        send(0, 2, -1, dx)
+    for rz in (6, 2):
+        send(0, rz, 0, 1)
+    for rz in (7, 1):
+        arrival(0, rz)
+        send(0, rz, 0, 1)
+    arrival(1, 0)
+    e_step(0)
+    e_step(1)
+    e_step(2)
+    for rx, rz in ((1, 1), (1, 7), (0, 3), (0, 5), (1, 2), (1, 6)):
+        arrival(rx, rz)
+    e_step(3)
+    for rx, rz in ((0, 4), (1, 3), (1, 5), (1, 4)):
+        arrival(rx, rz)
+    for u in range(4, NZ):
+        e_step(u)
 
     def lse_copy(dz, dx):
         slot = 2 * ((NZ - dz) % NZ) + dx
@@ -185,10 +191,10 @@
     for dz, dx in offsets:
         rz = (NZ - dz) % NZ
         term = lse_in[2 * rz + dx]
+        if dx:
+            term = jnp.stack([term[1], term[0]])
         if rz:
-            term = pltpu.roll(term, rz, 0)
-        if dx:
-            term = pltpu.roll(term, 2 * ROWS, 1)
+            term = pltpu.roll(term, rz, 1)
         terms.append(term)
     top = terms[0]
     for term in terms[1:]:
@@ -202,13 +208,11 @@
     core_part.start()
     core_part.wait_recv()
     other = part_in[...]
-    other = jnp.concatenate(
-        [pltpu.roll(other[:, : 2 * ROWS], ROWS, 1), pltpu.roll(other[:, 2 * ROWS :], ROWS, 1)], 1
-    )
+    other = pltpu.roll(other, ROWS, 2)
     top = jnp.maximum(mine, other)
     norm = top + jnp.log(jnp.exp(mine - top) + jnp.exp(other - top))
     lmax[...] = jnp.exp(lmax[...] - norm)
-    loglik = jnp.sum(jnp.sum(norm, 0, keepdims=True), 1, keepdims=True)
+    loglik = jnp.sum(jnp.sum(norm[0] + norm[1], 0, keepdims=True), 1, keepdims=True)
     cnt[pl.ds(4, 4), :] = jnp.broadcast_to(loglik, (4, CHUNK))
 
     def p1_copy(ch):
@@ -222,13 +226,14 @@
 
     def moments(ch):
         acc = jnp.zeros((CHUNK, 2 * D), F32)
-        number = jnp.zeros((CHUNK, D), F32)
+        number = jnp.zeros((CHUNK, PAIR), F32)
         comps = pl.ds(pl.multiple_of(ch * CHUNK, CHUNK), CHUNK)
-        for rz in range(NZ):
-            r = e_buf[rz, comps, :] * lmax[pl.ds(rz, 1), :]
-            number = number + r[:, :D] + r[:, D:]
+        for u, ((ax, az), (bx, bz)) in enumerate(UNITS):
+            scale = jnp.concatenate([lmax[ax, pl.ds(az, 1), :], lmax[bx, pl.ds(bz, 1), :]], 1)
+            r = e_buf[u, comps, :] * scale
+            number = number + r[:, :PAIR] + r[:, PAIR:]
             hi, lo = split(r)
-            acc = acc + dot_nn(hi, f_hi[rz]) + dot_nn(lo, f_hi[rz]) + dot_nn(hi, f_lo[rz])
+            acc = acc + dot_nn(hi, f_hi[u]) + dot_nn(lo, f_hi[u]) + dot_nn(hi, f_lo[u])
         cnt[pl.ds(ch, 1), :] = jnp.sum(number.T, 0, keepdims=True)
         sq, fi = acc[:, :D].T, acc[:, D:].T
         for half in range(2):
@@ -287,12 +292,11 @@
         nlw_ref[:, lanes] = jnp.log(denom / (TOTAL_ROWS + TOTAL_COMPS * PRIOR))
     ll_ref[...] = totals[4:5, :1] / (TOTAL_ROWS * D)
 
-    for dz in range(1, NZ):
-        z_copy(dz).wait_send()
-    for rz in range(NZ):
-        x_copy(rz).wait_send()
-        core_copy(rz, 0).wait_send()
-        core_copy(rz, 2).wait_send()
+    for copy in started:
+        copy.wait_send()
+    for rx in range(2):
+        for rz in range(NZ):
+            core_copy(rx, rz).wait_send()
     for dz, dx in offsets:
         lse_copy(dz, dx).wait_send()
     core_part.wait_send()
@@ -303,6 +307,15 @@
             p2_copy(ch, dy).wait_send()
     for dy in range(1, NY):
         c2_copy(dy).wait_send()
+
+
+def write(nm, nv, nlw, ll, nm_out, nv_out, nlw_out, ll_out, sem):
+    pairs = ((nm, nm_out), (nv, nv_out), (nlw, nlw_out), (ll, ll_out))
+    copies = [pltpu.make_async_copy(src, dst, sem.at[i]) for i, (src, dst) in enumerate(pairs)]
+    for copy in copies:
+        copy.start()
+    for copy in copies:
+        copy.wait()
 
 
 def local(descriptors, means, variances, log_weights):
@@ -316,24 +329,24 @@
             jax.ShapeDtypeStruct((1, COMPS), F32),
             jax.ShapeDtypeStruct((1, 1), F32),
         ),
-        in_specs=[pl.BlockSpec(memory_space=pl.ANY)] * 4,
+        in_specs=[pl.BlockSpec(memory_space=pltpu.HBM)] * 4,
         out_specs=(pl.BlockSpec(memory_space=pltpu.VMEM),) * 4,
         scratch_shapes=[
             vmem((D, COMPS), F32),
             vmem((D, COMPS), F32),
             vmem((1, COMPS), F32),
-            vmem((NZ, BLOCK, D), F32),
+            vmem((2, NZ, PAIR, D), F32),
             vmem((COMPS, 2 * D), BF16),
             vmem((COMPS, 2 * D), BF16),
             vmem((COMPS, D), F32),
             vmem((NZ, BLOCK, 2 * D), BF16),
             vmem((NZ, BLOCK, 2 * D), BF16),
             vmem((NZ, COMPS, BLOCK), F32),
-            vmem((NZ, BLOCK), F32),
-            vmem((NZ, BLOCK), F32),
-            vmem((2 * NZ, NZ, BLOCK), F32),
-            vmem((NZ, BLOCK), F32),
-            vmem((NZ, BLOCK), F32),
+            vmem((2, NZ, PAIR), F32),
+            vmem((2, NZ, PAIR), F32),
+            vmem((2 * NZ, 2, NZ, PAIR), F32),
+            vmem((2, NZ, PAIR), F32),
+            vmem((2, NZ, PAIR), F32),
             vmem((CHUNKS, 2, NY, 16, CHUNK), F32),
             vmem((CHUNKS, NY, 16, CHUNK), F32),
             vmem((CHUNKS, NY, 16, CHUNK), F32),
@@ -343,10 +356,10 @@
             vmem((8, CHUNK), F32),
             vmem((NY, 8, CHUNK), F32),
             sem((4,)),
-            sem((NZ,)),
-            sem((NZ,)),
-            sem((NZ, 4)),
-            sem((NZ, 4)),
+            sem((SENDS,)),
+            sem((2, NZ)),
+            sem((2, NZ)),
+            sem((2, NZ)),
             sem((2 * NZ,)),
             sem((2 * NZ,)),
             sem,
@@ -361,10 +374,18 @@
             sem((NY,)),
         ],
         compiler_params=pltpu.CompilerParams(
-            collective_id=0, has_side_effects=True, vmem_limit_bytes=40 * 2**20
+            collective_id=0, has_side_effects=True, vmem_limit_bytes=62 * 2**20
         ),
         name="em_step",
     )(descriptors, means, variances, log_weights.reshape(1, COMPS))
+    nm, nv, nlw, ll = pl.pallas_call(
+        write,
+        out_shape=tuple(jax.ShapeDtypeStruct(a.shape, F32) for a in (nm, nv, nlw, ll)),
+        in_specs=[pl.BlockSpec(memory_space=pltpu.HBM)] * 4,
+        out_specs=(pl.BlockSpec(memory_space=pltpu.HBM),) * 4,
+        scratch_shapes=[pltpu.SemaphoreType.DMA((4,))],
+        name="write",
+    )(nm, nv, nlw, ll)
     return nm, nv, nlw.reshape(COMPS), ll.reshape(())
 
 

time: 73.7 us -> 60.9 us (0.83)
  Pallas kernels: 65.9 us -> 60.1 us
  local copies, waits for them, and re-layouts: 5.12 us -> 0 us
  between operations: 2.4 us -> 0.64 us
    pallas_call x1, Pallas kernels: 65.9 us -> 57.3 us  [local(): pl.pallas_call(kernel, out_shape=(jax.ShapeDtypeStruct((8, COMPS), F32),...]
    unnamed x11 -> x0, local copies, waits for them, and re-layouts: 5.12 us -> none
    pallas_call x0 -> x1, Pallas kernels: none -> 2.81 us  [local(): pl.pallas_call(write, out_shape=tuple((jax.ShapeDtypeStruct(a.shape, F32)...]
where the time goes in v2:
time: 60.9 us; the launch traced here: 60.7 us
  Pallas kernels  60.1 us (99%)
  between operations  0.64 us (1%)
    pallas_call x1, Pallas kernels, local(): pl.pallas_call(kernel, out_shape=(jax.ShapeDtypeStruct((8, COMPS), F32),...  57.3 us
    pallas_call x1, Pallas kernels, local(): pl.pallas_call(write, out_shape=tuple((jax.ShapeDtypeStruct(a.shape, F32)...  2.81 us

profile of v2, /device:TPU:1, one launch (start us, length us, event | category | flops | bytes accessed | tf_op | source)
XLA Modules:
  0.0 60.7 jit_solution(12697305330341241986)
XLA Ops:
  0.6 57.3 %em_step.1 = (f32[8,512]{1,0:T(8,128)}, f32[8,512]{1,0:T(8,128)}, f32[1,512]{1,0:T(1,128)}, f32[1,1]{1,0:T(1,128)}) custom-call(f32[64,128]{1,0:T(8,128)} %x_hbm.1, f32[128,512]{1,0:T(8,128)} %means_hbm.1, f32[128,512]{1,0:T(8,128)} %var_hbm.1, f32[1,512]{1,0:T(1,128)} %bitcast.3), custom_call_target="tpu_custom_call" | custom-call | tf_op jit(solution)/shard_map/em_step/pallas_call | solution.py:324
  57.9 2.8 %write.1 = (f32[8,512]{1,0:T(8,128)}, f32[8,512]{1,0:T(8,128)}, f32[1,512]{1,0:T(1,128)}, f32[1,1]{1,0:T(1,128)}) custom-call(f32[8,512]{1,0:T(8,128)} %get-tuple-element.12.nm, f32[8,512]{1,0:T(8,128)} %get-tuple-element.13.nv, f32[1,512]{1,0:T(1,128)} %get-tuple-element.14.nlw, f32[1,1]{1,0:T(1,128)} %get-tuple-element.15.ll), custom_call_target="tpu_custom_call" | custom-call | tf_op jit(solution)/shard_map/write/pallas_call | solution.py:381

commit v3 on v2

--- a/solution.py
+++ b/solution.py
@@ -43,7 +43,7 @@
 
 def kernel(
     x_hbm, means_hbm, var_hbm, lw_hbm,
-    nm_ref, nv_ref, nlw_ref, ll_ref,
+    nm_ref, nv_ref, small_ref,
     means, var, lw, xg, p_hi, p_lo, off, f_hi, f_lo, e_buf, lse, lmax, lse_in, part, part_in,
     p1, p1_in, p2, p2_in, cnt, cnt_in, cnt2, cnt2_in,
     in_sem, g_s, g_r, gc_s, gc_r, l_s, l_r, lc_s, lc_r, p1_s, p1_r, p2_s, p2_r, c1_s, c1_r, c2_s, c2_r,
@@ -289,8 +289,9 @@
         nm_ref[:, lanes] = (first + PRIOR * m) / denom
         scatter = second - 2.0 * m * first + m * m * counts
         nv_ref[:, lanes] = (scatter + PRIOR * v) / denom
-        nlw_ref[:, lanes] = jnp.log(denom / (TOTAL_ROWS + TOTAL_COMPS * PRIOR))
-    ll_ref[...] = totals[4:5, :1] / (TOTAL_ROWS * D)
+        log_weights = jnp.log(denom / (TOTAL_ROWS + TOTAL_COMPS * PRIOR))
+        loglik = totals[4:5, :] / (TOTAL_ROWS * D)
+        small_ref[:, lanes] = jnp.concatenate([log_weights] * 4 + [loglik] * 4, 0)
 
     for copy in started:
         copy.wait_send()
@@ -309,28 +310,23 @@
         c2_copy(dy).wait_send()
 
 
-def write(nm, nv, nlw, ll, nm_out, nv_out, nlw_out, ll_out, sem):
-    pairs = ((nm, nm_out), (nv, nv_out), (nlw, nlw_out), (ll, ll_out))
-    copies = [pltpu.make_async_copy(src, dst, sem.at[i]) for i, (src, dst) in enumerate(pairs)]
-    for copy in copies:
-        copy.start()
-    for copy in copies:
-        copy.wait()
+def write(nm, nv, small, nm_out, nv_out, nlw_out, ll_out):
+    nm_out[...] = nm[...]
+    nv_out[...] = nv[...]
+    nlw_out[...] = small[pl.ds(0, 1), :]
+    ll_out[...] = small[pl.ds(4, 1), pl.ds(0, 1)]
 
 
 def local(descriptors, means, variances, log_weights):
+    operands = descriptors, means, variances, log_weights.reshape(1, COMPS)
     sem = pltpu.SemaphoreType.DMA
     vmem = pltpu.VMEM
-    nm, nv, nlw, ll = pl.pallas_call(
+    small = jax.ShapeDtypeStruct((8, COMPS), F32)
+    raw = pl.pallas_call(
         kernel,
-        out_shape=(
-            jax.ShapeDtypeStruct((8, COMPS), F32),
-            jax.ShapeDtypeStruct((8, COMPS), F32),
-            jax.ShapeDtypeStruct((1, COMPS), F32),
-            jax.ShapeDtypeStruct((1, 1), F32),
-        ),
+        out_shape=(small,) * 3,
         in_specs=[pl.BlockSpec(memory_space=pltpu.HBM)] * 4,
-        out_specs=(pl.BlockSpec(memory_space=pltpu.VMEM),) * 4,
+        out_specs=(pl.BlockSpec(memory_space=pltpu.VMEM),) * 3,
         scratch_shapes=[
             vmem((D, COMPS), F32),
             vmem((D, COMPS), F32),
@@ -374,18 +370,17 @@
             sem((NY,)),
         ],
         compiler_params=pltpu.CompilerParams(
-            collective_id=0, has_side_effects=True, vmem_limit_bytes=62 * 2**20
+            collective_id=0, has_side_effects=True, vmem_limit_bytes=40 * 2**20
         ),
         name="em_step",
-    )(descriptors, means, variances, log_weights.reshape(1, COMPS))
+    )(*(pltpu.with_memory_space_constraint(a, pltpu.HBM) for a in operands))
     nm, nv, nlw, ll = pl.pallas_call(
         write,
-        out_shape=tuple(jax.ShapeDtypeStruct(a.shape, F32) for a in (nm, nv, nlw, ll)),
-        in_specs=[pl.BlockSpec(memory_space=pltpu.HBM)] * 4,
-        out_specs=(pl.BlockSpec(memory_space=pltpu.HBM),) * 4,
-        scratch_shapes=[pltpu.SemaphoreType.DMA((4,))],
+        out_shape=(small, small, jax.ShapeDtypeStruct((1, COMPS), F32), jax.ShapeDtypeStruct((1, 1), F32)),
+        in_specs=[pl.BlockSpec(memory_space=pltpu.VMEM)] * 3,
+        out_specs=(pl.BlockSpec(memory_space=pltpu.VMEM),) * 4,
         name="write",
-    )(nm, nv, nlw, ll)
+    )(*raw)
     return nm, nv, nlw.reshape(COMPS), ll.reshape(())
 
 

time: 60.9 us -> 60.6 us (level)
  Pallas kernels: 60.1 us -> 58 us
  local copies, waits for them, and re-layouts: 0 us -> 1.79 us
    pallas_call x2, Pallas kernels: 60.1 us -> 58 us  [the longest x1 56.6 us: local(): pl.pallas_call(kernel, out_shape=(small,) * 3, in_specs=[pl.BlockSpec(mem...]
    unnamed x0 -> x6, local copies, waits for them, and re-layouts: none -> 1.79 us
where the time goes in v3:
time: 60.6 us; the launch traced here: 60.4 us
  Pallas kernels  58 us (96%)
  local copies, waits for them, and re-layouts  1.79 us (3%)
  between operations  0.65 us (1%)
    pallas_call x1, Pallas kernels, local(): pl.pallas_call(kernel, out_shape=(small,) * 3, in_specs=[pl.BlockSpec(mem...  56.6 us
    unnamed x6, local copies, waits for them, and re-layouts  1.79 us
    pallas_call x1, Pallas kernels, local(): pl.pallas_call(write, out_shape=(small, small, jax.ShapeDtypeStruct((1, C...  1.37 us

profile of v3, /device:TPU:1, one launch (start us, length us, event | category | flops | bytes accessed | tf_op | source)
XLA Modules:
  0.0 60.4 jit_solution(10020655383790069106)
XLA Ops:
  0.6 56.6 %em_step.1 = (f32[8,512]{1,0:T(8,128)S(1)}, f32[8,512]{1,0:T(8,128)S(1)}, f32[8,512]{1,0:T(8,128)S(1)}) custom-call(f32[64,128]{1,0:T(8,128)} %x_hbm.1, f32[128,512]{1,0:T(8,128)} %means_hbm.1, f32[128,512]{1,0:T(8,128)} %var_hbm.1, f32[1,512]{1,0:T(1,128)} %bitcast.3), custom_call_target="tpu_custom_call" | custom-call | tf_op jit(solution)/shard_map/em_step/pallas_call | solution.py:325
  57.3 0.0 copy-start
  57.3 0.6 copy-done
  57.9 0.0 copy-start.1
  57.9 0.6 copy-done.1
  58.5 0.0 copy-start.2
  58.5 0.6 copy-done.2
  59.1 1.4 %write.1 = (f32[8,512]{1,0:T(8,128)}, f32[8,512]{1,0:T(8,128)}, f32[1,512]{1,0:T(1,128)}, f32[1,1]{1,0:T(1,128)}) custom-call(f32[8,512]{1,0:T(8,128)} %copy-done, f32[8,512]{1,0:T(8,128)} %copy-done.1, f32[8,512]{1,0:T(8,128)} %copy-done.2), custom_call_target="tpu_custom_call" | custom-call | tf_op jit(solution)/shard_map/write/pallas_call | solution.py:377
Async XLA Ops:
  57.3 0.6 copy-start
  57.9 0.6 copy-start.1
  58.5 0.6 copy-start.2

commit v4 on v3

--- a/solution.py
+++ b/solution.py
@@ -46,7 +46,7 @@
     nm_ref, nv_ref, small_ref,
     means, var, lw, xg, p_hi, p_lo, off, f_hi, f_lo, e_buf, lse, lmax, lse_in, part, part_in,
     p1, p1_in, p2, p2_in, cnt, cnt_in, cnt2, cnt2_in,
-    in_sem, g_s, g_r, gc_s, gc_r, l_s, l_r, lc_s, lc_r, p1_s, p1_r, p2_s, p2_r, c1_s, c1_r, c2_s, c2_r,
+    hello, in_sem, g_s, g_r, gc_s, gc_r, l_s, l_r, lc_s, lc_r, p1_s, p1_r, p2_s, p2_r, c1_s, c1_r, c2_s, c2_r,
 ):
     d = lax.axis_index("dp")
     c = lax.axis_index("comp")
@@ -76,12 +76,10 @@
         copy.start()
 
     barrier = pltpu.get_barrier_semaphore()
-    peers = [at(dz, dx, 0) for dz in range(NZ) for dx in range(2) if dz or dx] + [at(0, 0, 1), xlo_peer]
-    peers += [y_peer(dy) for dy in range(1, NY)]
+    peers = [at(dz, 0, 0) for dz in (1, 7, 2, 6)] + [at(0, 1, 0), at(0, 0, 1), xlo_peer]
+    peers += [y_peer(dy) for dy in (1, 7, 2, 6)]
     for peer in peers:
         pl.semaphore_signal(barrier, inc=1, device_id=peer, device_id_type=MESH)
-    for copy in local_in:
-        copy.wait()
     pl.semaphore_wait(barrier, len(peers))
 
     def block(rx, rz, rc):
@@ -94,17 +92,21 @@
 
     started = []
 
+    def held(rx, rz):
+        own = isinstance(rz, int) and (rx, rz) == (0, 0)
+        return x_hbm if own else block(rx, rz, 0)
+
     def send(rx, rz, dz, dx):
         number = len(started)
         to_x, to_z = 1 - rx if dx else rx, (rz - dz) % NZ
         copy = remote(
-            block(rx, rz, 0), block(to_x, to_z, 0), g_s.at[number], g_r.at[to_x, to_z], at(dz, dx, 0)
+            held(rx, rz), block(to_x, to_z, 0), g_s.at[number], g_r.at[to_x, to_z], at(dz, dx, 0)
         )
         copy.start()
         started.append(copy)
 
     def core_copy(rx, rz):
-        return remote(block(rx, rz, 0), block(rx, rz, 1), gc_s.at[rx, rz], gc_r.at[rx, rz], at(0, 0, 1))
+        return remote(held(rx, rz), block(rx, rz, 1), gc_s.at[rx, rz], gc_r.at[rx, rz], at(0, 0, 1))
 
     def arrival(rx, rz):
         remote(block(rx, rz, 0), block(rx, rz, 0), g_s.at[0], g_r.at[rx, rz], at(0, 1, 0)).wait_recv()
@@ -114,6 +116,10 @@
         send(0, 0, dz, 0)
     send(0, 0, 0, 1)
     core_copy(0, 0).start()
+    for number, dy in enumerate((2, 6)):
+        pl.semaphore_signal(hello.at[number], inc=1, device_id=y_peer(dy), device_id_type=MESH)
+    for copy in local_in:
+        copy.wait()
 
     prec = 1.0 / var[...]
     lin = means[...] * prec
@@ -154,6 +160,7 @@
 
     side = 1 - 2 * core
     far = (NZ - 2 * side) % NZ
+    arrival(1, 0)
     arrival(0, 6)
     arrival(0, 2)
     send(0, far, 2 * side, 1)
@@ -166,17 +173,18 @@
     for rz in (7, 1):
         arrival(0, rz)
         send(0, rz, 0, 1)
-    arrival(1, 0)
     e_step(0)
     e_step(1)
     e_step(2)
     for rx, rz in ((1, 1), (1, 7), (0, 3), (0, 5), (1, 2), (1, 6)):
         arrival(rx, rz)
     e_step(3)
+    e_step(4)
     for rx, rz in ((0, 4), (1, 3), (1, 5), (1, 4)):
         arrival(rx, rz)
-    for u in range(4, NZ):
-        e_step(u)
+    e_step(5)
+    e_step(6)
+    e_step(7)
 
     def lse_copy(dz, dx):
         slot = 2 * ((NZ - dz) % NZ) + dx
@@ -249,6 +257,8 @@
         for dy in (4, 3, 5, 2, 6, 1, 7):
             p2_copy(ch, dy).start()
 
+    for number in range(2):
+        pl.semaphore_wait(hello.at[number], 1)
     moments(0)
 
     def moment_step(ch, carry):
@@ -351,6 +361,7 @@
             vmem((8, CHUNK), F32),
             vmem((8, CHUNK), F32),
             vmem((NY, 8, CHUNK), F32),
+            pltpu.SemaphoreType.REGULAR((2,)),
             sem((4,)),
             sem((SENDS,)),
             sem((2, NZ)),
@@ -379,6 +390,7 @@
         out_shape=(small, small, jax.ShapeDtypeStruct((1, COMPS), F32), jax.ShapeDtypeStruct((1, 1), F32)),
         in_specs=[pl.BlockSpec(memory_space=pltpu.VMEM)] * 3,
         out_specs=(pl.BlockSpec(memory_space=pltpu.VMEM),) * 4,
+        compiler_params=pltpu.CompilerParams(vmem_limit_bytes=4 * 2**20),
         name="write",
     )(*raw)
     return nm, nv, nlw.reshape(COMPS), ll.reshape(())

time: 60.6 us -> 55.8 us (0.921)
  Pallas kernels: 58 us -> 55.1 us
  local copies, waits for them, and re-layouts: 1.79 us -> 0 us
    pallas_call x1, Pallas kernels: 56.6 us -> 54.4 us  [local(): pl.pallas_call(kernel, out_shape=(small,) * 3, in_specs=[pl.BlockSpec(mem...]
    unnamed x6 -> x0, local copies, waits for them, and re-layouts: 1.79 us -> none
    pallas_call x1, Pallas kernels: 1.37 us -> 0.62 us  [local(): pl.pallas_call(write, out_shape=(small, small, jax.ShapeDtypeStruct((1, C...]
where the time goes in v4:
time: 55.8 us; the launch traced here: 55.7 us
  Pallas kernels  55.1 us (99%)
  between operations  0.64 us (1%)
    pallas_call x1, Pallas kernels, local(): pl.pallas_call(kernel, out_shape=(small,) * 3, in_specs=[pl.BlockSpec(mem...  54.4 us

profile of v4, /device:TPU:1, one launch (start us, length us, event | category | flops | bytes accessed | tf_op | source)
XLA Modules:
  0.0 55.7 jit_solution(289076991355190471)
XLA Ops:
  0.6 54.4 %em_step.1 = (f32[8,512]{1,0:T(8,128)S(1)}, f32[8,512]{1,0:T(8,128)S(1)}, f32[8,512]{1,0:T(8,128)S(1)}) custom-call(f32[64,128]{1,0:T(8,128)} %x_hbm.1, f32[128,512]{1,0:T(8,128)} %means_hbm.1, f32[128,512]{1,0:T(8,128)} %var_hbm.1, f32[1,512]{1,0:T(1,128)} %bitcast.3), custom_call_target="tpu_custom_call" | custom-call | tf_op jit(solution)/shard_map/em_step/pallas_call | solution.py:335
  55.1 0.6 %write.1 = (f32[8,512]{1,0:T(8,128)}, f32[8,512]{1,0:T(8,128)}, f32[1,512]{1,0:T(1,128)}, f32[1,1]{1,0:T(1,128)}) custom-call(f32[8,512]{1,0:T(8,128)S(1)} %get-tuple-element.11.nm, f32[8,512]{1,0:T(8,128)S(1)} %get-tuple-element.12.nv, f32[8,512]{1,0:T(8,128)S(1)} %get-tuple-element.13.small), custom_call_target="tpu_custom_call" | custom-call | tf_op jit(solution)/shard_map/write/pallas_call | solution.py:388

commit v5 on v4

v5 whole, which is shorter than its diff:
```python
import math

import jax
import jax.numpy as jnp
from jax import lax
from jax.experimental import pallas as pl
from jax.experimental.pallas import tpu as pltpu
from jax.sharding import PartitionSpec as P

LOG_TWO_PI = math.log(2.0 * math.pi)
PRIOR = 1.0
MESH = pl.DeviceIdType.MESH
D = 128
ROWS = 64
NZ, NY = 8, 8
COMPS = 512
PAIR = 2 * ROWS
BLOCK = 2 * PAIR
UNITS = ((0, 1), (7, 2), (6, 3), (5, 4))
STEPS = len(UNITS)
SENDS = 15
FAR_FIRST = (4, 3, 5, 2, 6, 1, 7)
CHUNK = 128
CHUNKS = COMPS // CHUNK
LAST = CHUNKS - 1
TOTAL_ROWS = 32768
TOTAL_COMPS = 16384
F32, BF16 = jnp.float32, jnp.bfloat16


def split(a):
    hi = a.astype(BF16)
    return hi, (a - hi.astype(F32)).astype(BF16)


def dot_nt(a, b):
    return lax.dot_general(a, b, (((1,), (1,)), ((), ())), preferred_element_type=F32)


def dot_nn(a, b):
    return lax.dot_general(a, b, (((1,), (0,)), ((), ())), preferred_element_type=F32)


def kernel(
    x_hbm, means_hbm, var_hbm, lw_hbm,
    nm_ref, nv_ref, small_ref,
    means, var, lw, xg, p_hi, p_lo, off, f_hi, f_lo, e_buf, lse, lmax, lse_in, half, half_in, hcnt, hcnt_in,
    p1, p1_in, p2, p2_in, p3_in, cnt, cnt_in, cnt2, cnt2_in,
    hello, in_sem, g_s, g_r, a_s, a_r, l_s, l_r, h_s, h_r, hc_s, hc_r,
    p1_s, p1_r, p2_s, p2_r, p3_s, p3_r, c1_s, c1_r, c2_s, c2_r,
):
    d = lax.axis_index("dp")
    c = lax.axis_index("comp")
    y, xlo = d // 2, d % 2
    core = c % 2
    xhi = (c // 2) % 2
    z = c // 4

    def at(dz, dx, dc):
        nz = (z + dz) % NZ
        nx = 1 - xhi if dx else xhi
        nc = 1 - core if dc else core
        return (d, nz * 4 + nx * 2 + nc)

    def y_peer(dy):
        return (((y + dy) % NY) * 2 + xlo, c)

    xlo_peer = (y * 2 + 1 - xlo, c)

    local_in = [
        pltpu.make_async_copy(means_hbm, means.at[0], in_sem.at[0]),
        pltpu.make_async_copy(var_hbm, var.at[0], in_sem.at[1]),
        pltpu.make_async_copy(lw_hbm, lw.at[0], in_sem.at[2]),
        pltpu.make_async_copy(x_hbm, xg.at[0, pl.ds(0, ROWS)], in_sem.at[3]),
    ]
    for copy in local_in:
        copy.start()

    barrier = pltpu.get_barrier_semaphore()
    peers = [at(dz, 0, 0) for dz in (1, 7, 2, 6)] + [at(0, 1, 0), at(0, 0, 1), xlo_peer]
    peers += [y_peer(dy) for dy in (1, 7, 2, 6)]
    for peer in peers:
        pl.semaphore_signal(barrier, inc=1, device_id=peer, device_id_type=MESH)
    pl.semaphore_wait(barrier, len(peers))

    def block(rx, rz):
        return xg.at[rz, pl.ds(ROWS * rx, ROWS)]

    def remote(src, dst, send, recv, peer):
        return pltpu.make_async_remote_copy(
            src_ref=src, dst_ref=dst, send_sem=send, recv_sem=recv, device_id=peer, device_id_type=MESH
        )

    started = []

    def held(rx, rz):
        own = isinstance(rz, int) and (rx, rz) == (0, 0)
        return x_hbm if own else block(rx, rz)

    def send(rx, rz, dz, dx):
        number = len(started)
        to_x, to_z = 1 - rx if dx else rx, (rz - dz) % NZ
        copy = remote(
            held(rx, rz), block(to_x, to_z), g_s.at[number], g_r.at[to_x, to_z], at(dz, dx, 0)
        )
        copy.start()
        started.append(copy)

    def arrival(rx, rz):
        remote(block(rx, rz), block(rx, rz), g_s.at[0], g_r.at[rx, rz], at(0, 1, 0)).wait_recv()

    for dz in (2, 6, 1, 7):
        send(0, 0, dz, 0)
    send(0, 0, 0, 1)
    swap = [
        remote(src, dst.at[1], a_s.at[i], a_r.at[i], at(0, 0, 1))
        for i, (src, dst) in enumerate(((var_hbm, var), (means_hbm, means), (lw_hbm, lw)))
    ]
    for copy in swap:
        copy.start()
    for number, dy in enumerate((2, 6)):
        pl.semaphore_signal(hello.at[number], inc=1, device_id=y_peer(dy), device_id_type=MESH)
    for copy in local_in:
        copy.wait()

    def component_side(side):
        v, m = var[side], means[side]
        comps = pl.ds(COMPS * side, COMPS)
        prec = 1.0 / v
        lin = m * prec
        offset = (
            lw[side]
            - 0.5 * jnp.sum(m * lin, 0, keepdims=True)
            - 0.5 * jnp.sum(jnp.log(v), 0, keepdims=True)
            - 0.5 * D * LOG_TWO_PI
        )
        off[comps, :] = jnp.broadcast_to(offset, (D, COMPS)).T
        for part_number, a in enumerate((-0.5 * prec, lin)):
            hi, lo = split(a.T)
            p_hi[comps, pl.ds(D * part_number, D)] = hi
            p_lo[comps, pl.ds(D * part_number, D)] = lo

    component_side(0)

    def e_step(u):
        az, bz = UNITS[u]
        rows = jnp.concatenate([xg[az], xg[bz]], 0)
        sq_hi, sq_lo = split(rows * rows)
        x_hi, x_lo = split(rows)
        f_hi[u, :, pl.ds(0, D)] = sq_hi
        f_hi[u, :, pl.ds(D, D)] = x_hi
        f_lo[u, :, pl.ds(0, D)] = sq_lo
        f_lo[u, :, pl.ds(D, D)] = x_lo
        fh, fl = f_hi[u], f_lo[u]
        scores = []
        for side in range(2):
            comps = pl.ds(COMPS * side, COMPS)
            s = dot_nt(p_hi[comps], fh) + dot_nt(p_lo[comps], fh) + dot_nt(p_hi[comps], fl)
            scores.append(s + jnp.concatenate([off[comps, :], off[comps, :]], 1))
        top = jnp.maximum(jnp.max(scores[0], 0, keepdims=True), jnp.max(scores[1], 0, keepdims=True))
        total = jnp.zeros_like(top)
        for side in range(2):
            e = jnp.exp(scores[side] - top)
            e_buf[u, pl.ds(COMPS * side, COMPS), :] = e
            total = total + jnp.sum(e, 0, keepdims=True)
        total = top + jnp.log(total)
        for number, rz in enumerate(UNITS[u]):
            lanes = slice(number * PAIR, (number + 1) * PAIR)
            lmax[pl.ds(rz, 1), :] = top[:, lanes]
            lse[pl.ds(rz, 1), :] = total[:, lanes]

    side = 1 - 2 * core
    far = (NZ - 2 * side) % NZ
    arrival(1, 0)
    arrival(0, 6)
    arrival(0, 2)
    send(0, far, 2 * side, 1)
    send(0, far, 2 * side, 0)
    for dx in (1, 0):
        send(0, 6, 1, dx)
        send(0, 2, -1, dx)
    for rz in (6, 2):
        send(0, rz, 0, 1)
    for rz in (7, 1):
        arrival(0, rz)
        send(0, rz, 0, 1)
    for copy in swap:
        copy.wait_recv()
    component_side(1)
    arrival(1, 1)
    e_step(0)
    arrival(1, 7)
    arrival(1, 2)
    e_step(1)
    for rx, rz in ((1, 6), (0, 3), (1, 3)):
        arrival(rx, rz)
    e_step(2)
    for rx, rz in ((0, 5), (0, 4), (1, 5), (1, 4)):
        arrival(rx, rz)
    e_step(3)

    def lse_copy(dz, dx):
        slot = 2 * ((NZ - dz) % NZ) + dx
        return remote(lse, lse_in.at[slot], l_s.at[2 * dz + dx], l_r.at[slot], at(dz, dx, 0))

    offsets = [(dz, dx) for dz in (4, 3, 5, 2, 6, 1, 7, 0) for dx in (1, 0) if (dz, dx) != (0, 0)]
    for dz, dx in offsets:
        lse_copy(dz, dx).start()
    for dz, dx in offsets:
        lse_copy(dz, dx).wait_recv()
    terms = [lse[...]]
    for dz, dx in offsets:
        rz = (NZ - dz) % NZ
        term = lse_in[2 * rz + dx]
        if dx:
            term = pltpu.roll(term, ROWS, 1)
        if rz:
            term = pltpu.roll(term, rz, 0)
        terms.append(term)
    top = terms[0]
    for term in terms[1:]:
        top = jnp.maximum(top, term)
    total = jnp.exp(terms[0] - top)
    for term in terms[1:]:
        total = total + jnp.exp(term - top)
    norm = top + jnp.log(total)
    lmax[...] = jnp.exp(lmax[...] - norm)
    loglik = jnp.sum(jnp.sum(norm, 0, keepdims=True), 1, keepdims=True)
    for ref in (cnt, hcnt):
        ref[pl.ds(4, 4), :] = jnp.broadcast_to(loglik, (4, CHUNK))

    def p1_copy(ch):
        return remote(p1.at[ch, 1 - xlo], p1_in.at[ch], p1_s.at[ch], p1_r.at[ch], xlo_peer)

    def p2_copy(ch, dy):
        slot = (NY - dy) % NY
        return remote(
            p2.at[ch, (y + dy) % NY], p2_in.at[ch, slot], p2_s.at[ch, dy], p2_r.at[ch, slot], y_peer(dy)
        )

    def p3_copy(dy, dx):
        slot = 2 * ((NY - dy) % NY) + dx
        peer_x = 1 - xlo if dx else xlo
        peer_y = (y + dy) % NY
        return remote(
            p1.at[LAST, peer_x, peer_y], p3_in.at[slot], p3_s.at[2 * dy + dx], p3_r.at[slot], (peer_y * 2 + peer_x, c)
        )

    def half_copy(ch):
        return remote(half.at[ch], half_in.at[ch], h_s.at[ch], h_r.at[ch], at(0, 0, 1))

    def partial_moments(side, ch):
        acc = jnp.zeros((CHUNK, 2 * D), F32)
        number = jnp.zeros((CHUNK, PAIR), F32)
        comps = pl.ds(COMPS * side + CHUNK * ch, CHUNK)
        for u, (az, bz) in enumerate(UNITS):
            scale = jnp.concatenate([lmax[pl.ds(az, 1), :], lmax[pl.ds(bz, 1), :]], 1)
            r = e_buf[u, comps, :] * scale
            number = number + r[:, :PAIR] + r[:, PAIR:]
            hi, lo = split(r)
            acc = acc + dot_nn(hi, f_hi[u]) + dot_nn(lo, f_hi[u]) + dot_nn(hi, f_lo[u])
        return acc, jnp.sum(number.T, 0, keepdims=True)

    def moments(ch):
        acc, number = partial_moments(0, ch)
        cnt[pl.ds(ch, 1), :] = number
        half_copy(ch).wait_recv()
        acc = acc + half_in[ch]
        sq, fi = acc[:, :D].T, acc[:, D:].T
        for side in range(2):
            for ny in range(NY):
                at_row = 16 * ny + 8 * side
                p1[ch, side, ny, pl.ds(0, 8), :] = sq[at_row : at_row + 8]
                p1[ch, side, ny, pl.ds(8, 8), :] = fi[at_row : at_row + 8]

    def pass_on(ch):
        p1_copy(ch).wait_recv()
        p2[ch] = p1[ch, xlo] + p1_in[ch]
        for dy in FAR_FIRST:
            p2_copy(ch, dy).start()

    for ch in range(CHUNKS):
        half[ch], number = partial_moments(1, ch)
        hcnt[pl.ds(ch, 1), :] = number
        half_copy(ch).start()
    for number in range(2):
        pl.semaphore_wait(hello.at[number], 1)
    hc = remote(hcnt, hcnt_in, hc_s, hc_r, at(0, 0, 1))
    hc.start()
    for ch in range(LAST):
        moments(ch)
        p1_copy(ch).start()
    moments(LAST)
    for dy in FAR_FIRST:
        p3_copy(dy, 0).start()
    hc.wait_recv()
    cnt[...] = cnt[...] + hcnt_in[...]
    c1 = remote(cnt, cnt_in, c1_s, c1_r, xlo_peer)
    c1.start()
    pass_on(0)
    pass_on(1)
    for dy in FAR_FIRST + (0,):
        p3_copy(dy, 1).start()
    c1.wait_recv()
    cnt2[...] = cnt[...] + cnt_in[...]

    def c2_copy(dy):
        slot = (NY - dy) % NY
        return remote(cnt2, cnt2_in.at[slot], c2_s.at[dy], c2_r.at[slot], y_peer(dy))

    for dy in FAR_FIRST:
        c2_copy(dy).start()
    pass_on(2)
    others = [(dy, dx) for dy in range(NY) for dx in range(2) if dy or dx]
    sums = [p2[ch, y] for ch in range(LAST)] + [p1[LAST, xlo, y]]
    for dy, dx in others:
        p3_copy(dy, dx).wait_recv()
        sums[LAST] = sums[LAST] + p3_in[2 * ((NY - dy) % NY) + dx]
    for ch in range(LAST):
        for dy in range(1, NY):
            p2_copy(ch, dy).wait_recv()
    for dy in range(1, NY):
        c2_copy(dy).wait_recv()
    totals = cnt2[...]
    for dy in range(1, NY):
        totals = totals + cnt2_in[dy]
        for ch in range(LAST):
            sums[ch] = sums[ch] + p2_in[ch, dy]
    own = pl.ds(pl.multiple_of(d * 8, 8), 8)
    for ch in range(CHUNKS):
        lanes = pl.ds(ch * CHUNK, CHUNK)
        counts = totals[ch : ch + 1, :]
        denom = counts + PRIOR
        second, first = sums[ch][:8], sums[ch][8:]
        m, v = means[0, own, lanes], var[0, own, lanes]
        nm_ref[:, lanes] = (first + PRIOR * m) / denom
        scatter = second - 2.0 * m * first + m * m * counts
        nv_ref[:, lanes] = (scatter + PRIOR * v) / denom
        log_weights = jnp.log(denom / (TOTAL_ROWS + TOTAL_COMPS * PRIOR))
        loglik = totals[4:5, :] / (TOTAL_ROWS * D)
        small_ref[:, lanes] = jnp.concatenate([log_weights] * 4 + [loglik] * 4, 0)

    for copy in started + swap + [hc, c1]:
        copy.wait_send()
    for dz, dx in offsets:
        lse_copy(dz, dx).wait_send()
    for ch in range(CHUNKS):
        half_copy(ch).wait_send()
    for ch in range(LAST):
        p1_copy(ch).wait_send()
        for dy in range(1, NY):
            p2_copy(ch, dy).wait_send()
    for dy, dx in others:
        p3_copy(dy, dx).wait_send()
    for dy in range(1, NY):
        c2_copy(dy).wait_send()


def write(nm, nv, small, nm_out, nv_out, nlw_out, ll_out):
    nm_out[...] = nm[...]
    nv_out[...] = nv[...]
    nlw_out[...] = small[pl.ds(0, 1), :]
    ll_out[...] = small[pl.ds(4, 1), pl.ds(0, 1)]


def local(descriptors, means, variances, log_weights):
    operands = descriptors, means, variances, log_weights.reshape(1, COMPS)
    sem = pltpu.SemaphoreType.DMA
    vmem = pltpu.VMEM
    small = jax.ShapeDtypeStruct((8, COMPS), F32)
    raw = pl.pallas_call(
        kernel,
        out_shape=(small,) * 3,
        in_specs=[pl.BlockSpec(memory_space=pltpu.HBM)] * 4,
        out_specs=(pl.BlockSpec(memory_space=pltpu.VMEM),) * 3,
        scratch_shapes=[
            vmem((2, D, COMPS), F32),
            vmem((2, D, COMPS), F32),
            vmem((2, 1, COMPS), F32),
            vmem((NZ, PAIR, D), F32),
            vmem((2 * COMPS, 2 * D), BF16),
            vmem((2 * COMPS, 2 * D), BF16),
            vmem((2 * COMPS, D), F32),
            vmem((STEPS, BLOCK, 2 * D), BF16),
            vmem((STEPS, BLOCK, 2 * D), BF16),
            vmem((STEPS, 2 * COMPS, BLOCK), F32),
            vmem((NZ, PAIR), F32),
            vmem((NZ, PAIR), F32),
            vmem((2 * NZ, NZ, PAIR), F32),
            vmem((CHUNKS, CHUNK, 2 * D), F32),
            vmem((CHUNKS, CHUNK, 2 * D), F32),
            vmem((8, CHUNK), F32),
            vmem((8, CHUNK), F32),
            vmem((CHUNKS, 2, NY, 16, CHUNK), F32),
            vmem((LAST, NY, 16, CHUNK), F32),
            vmem((LAST, NY, 16, CHUNK), F32),
            vmem((LAST, NY, 16, CHUNK), F32),
            vmem((2 * NY, 16, CHUNK), F32),
            vmem((8, CHUNK), F32),
            vmem((8, CHUNK), F32),
            vmem((8, CHUNK), F32),
            vmem((NY, 8, CHUNK), F32),
            pltpu.SemaphoreType.REGULAR((2,)),
            sem((4,)),
            sem((SENDS,)),
            sem((2, NZ)),
            sem((3,)),
            sem((3,)),
            sem((2 * NZ,)),
            sem((2 * NZ,)),
            sem((CHUNKS,)),
            sem((CHUNKS,)),
            sem,
            sem,
            sem((LAST,)),
            sem((LAST,)),
            sem((LAST, NY)),
            sem((LAST, NY)),
            sem((2 * NY,)),
            sem((2 * NY,)),
            sem,
            sem,
            sem((NY,)),
            sem((NY,)),
        ],
        compiler_params=pltpu.CompilerParams(
            collective_id=0, has_side_effects=True, vmem_limit_bytes=40 * 2**20
        ),
        name="em_step",
    )(*(pltpu.with_memory_space_constraint(a, pltpu.HBM) for a in operands))
    nm, nv, nlw, ll = pl.pallas_call(
        write,
        out_shape=(small, small, jax.ShapeDtypeStruct((1, COMPS), F32), jax.ShapeDtypeStruct((1, 1), F32)),
        in_specs=[pl.BlockSpec(memory_space=pltpu.VMEM)] * 3,
        out_specs=(pl.BlockSpec(memory_space=pltpu.VMEM),) * 4,
        compiler_params=pltpu.CompilerParams(vmem_limit_bytes=4 * 2**20),
        name="write",
    )(*raw)
    return nm, nv, nlw.reshape(COMPS), ll.reshape(())


def solution(mesh):
    placed = (P(("dp", "comp"), None), P(None, "comp"), P(None, "comp"), P("comp"))
    return jax.shard_map(
        local,
        mesh=mesh,
        in_specs=placed,
        out_specs=(P("dp", "comp"), P("dp", "comp"), P("comp"), P()),
        check_vma=False,
    )
```

time: 55.8 us -> 50.3 us (0.901)
  Pallas kernels: 55.1 us -> 49.1 us
    pallas_call x1, Pallas kernels: 54.4 us -> 48.5 us  [local(): pl.pallas_call(kernel, out_shape=(small,) * 3, in_specs=[pl.BlockSpec(mem...]
where the time goes in v5:
time: 50.3 us; the launch traced here: 49.7 us
  Pallas kernels  49.1 us (98%)
  between operations  0.64 us (1%)
    pallas_call x1, Pallas kernels, local(): pl.pallas_call(kernel, out_shape=(small,) * 3, in_specs=[pl.BlockSpec(mem...  48.5 us

profile of v5, /device:TPU:1, one launch (start us, length us, event | category | flops | bytes accessed | tf_op | source)
XLA Modules:
  0.0 49.7 jit_solution(9629576349572329944)
XLA Ops:
  0.6 48.5 %em_step.1 = (f32[8,512]{1,0:T(8,128)S(1)}, f32[8,512]{1,0:T(8,128)S(1)}, f32[8,512]{1,0:T(8,128)S(1)}) custom-call(f32[64,128]{1,0:T(8,128)} %x_hbm.1, f32[128,512]{1,0:T(8,128)} %means_hbm.1, f32[128,512]{1,0:T(8,128)} %var_hbm.1, f32[1,512]{1,0:T(1,128)} %bitcast.3), custom_call_target="tpu_custom_call" | custom-call | tf_op jit(solution)/shard_map/em_step/pallas_call | solution.py:371
  49.1 0.6 %write.1 = (f32[8,512]{1,0:T(8,128)}, f32[8,512]{1,0:T(8,128)}, f32[1,512]{1,0:T(1,128)}, f32[1,1]{1,0:T(1,128)}) custom-call(f32[8,512]{1,0:T(8,128)S(1)} %get-tuple-element.11.nm, f32[8,512]{1,0:T(8,128)S(1)} %get-tuple-element.12.nv, f32[8,512]{1,0:T(8,128)S(1)} %get-tuple-element.13.small), custom_call_target="tpu_custom_call" | custom-call | tf_op jit(solution)/shard_map/write/pallas_call | solution.py:431

commit v6 on v5

--- a/solution.py
+++ b/solution.py
@@ -8,6 +8,7 @@
 from jax.sharding import PartitionSpec as P
 
 LOG_TWO_PI = math.log(2.0 * math.pi)
+LOG_TWO = math.log(2.0)
 PRIOR = 1.0
 MESH = pl.DeviceIdType.MESH
 D = 128
@@ -15,8 +16,13 @@
 NZ, NY = 8, 8
 COMPS = 512
 PAIR = 2 * ROWS
-BLOCK = 2 * PAIR
-UNITS = ((0, 1), (7, 2), (6, 3), (5, 4))
+BLOCK = 4 * ROWS
+UNITS = (
+    ((0, 0), (1, 0), (0, 1), (0, 7)),
+    ((0, 2), (1, 1), (0, 6), (1, 7)),
+    ((0, 3), (1, 2), (0, 5), (1, 6)),
+    ((0, 4), (1, 4), (1, 3), (1, 5)),
+)
 STEPS = len(UNITS)
 SENDS = 15
 FAR_FIRST = (4, 3, 5, 2, 6, 1, 7)
@@ -44,7 +50,7 @@
 def kernel(
     x_hbm, means_hbm, var_hbm, lw_hbm,
     nm_ref, nv_ref, small_ref,
-    means, var, lw, xg, p_hi, p_lo, off, f_hi, f_lo, e_buf, lse, lmax, lse_in, half, half_in, hcnt, hcnt_in,
+    means, var, lw, xg, p_hi, p_lo, off, f_hi, f_lo, e_buf, lse, scale, lse_in, half, half_in, hcnt, hcnt_in,
     p1, p1_in, p2, p2_in, p3_in, cnt, cnt_in, cnt2, cnt2_in,
     hello, in_sem, g_s, g_r, a_s, a_r, l_s, l_r, h_s, h_r, hc_s, hc_r,
     p1_s, p1_r, p2_s, p2_r, p3_s, p3_r, c1_s, c1_r, c2_s, c2_r,
@@ -134,17 +140,16 @@
             - 0.5 * jnp.sum(jnp.log(v), 0, keepdims=True)
             - 0.5 * D * LOG_TWO_PI
         )
-        off[comps, :] = jnp.broadcast_to(offset, (D, COMPS)).T
+        off[comps, :] = jnp.broadcast_to(offset * (1.0 / LOG_TWO), (D, COMPS)).T
         for part_number, a in enumerate((-0.5 * prec, lin)):
-            hi, lo = split(a.T)
+            hi, lo = split((a * (1.0 / LOG_TWO)).T)
             p_hi[comps, pl.ds(D * part_number, D)] = hi
             p_lo[comps, pl.ds(D * part_number, D)] = lo
 
     component_side(0)
 
     def e_step(u):
-        az, bz = UNITS[u]
-        rows = jnp.concatenate([xg[az], xg[bz]], 0)
+        rows = jnp.concatenate([block(rx, rz)[...] for rx, rz in UNITS[u]], 0)
         sq_hi, sq_lo = split(rows * rows)
         x_hi, x_lo = split(rows)
         f_hi[u, :, pl.ds(0, D)] = sq_hi
@@ -160,14 +165,13 @@
         top = jnp.maximum(jnp.max(scores[0], 0, keepdims=True), jnp.max(scores[1], 0, keepdims=True))
         total = jnp.zeros_like(top)
         for side in range(2):
-            e = jnp.exp(scores[side] - top)
+            e = jnp.exp2(scores[side] - top)
             e_buf[u, pl.ds(COMPS * side, COMPS), :] = e
             total = total + jnp.sum(e, 0, keepdims=True)
-        total = top + jnp.log(total)
-        for number, rz in enumerate(UNITS[u]):
-            lanes = slice(number * PAIR, (number + 1) * PAIR)
-            lmax[pl.ds(rz, 1), :] = top[:, lanes]
-            lse[pl.ds(rz, 1), :] = total[:, lanes]
+        total = top + jnp.log2(total)
+        scale[pl.ds(u, 1), :] = top
+        for number, (rx, rz) in enumerate(UNITS[u]):
+            lse[pl.ds(rz, 1), pl.ds(ROWS * rx, ROWS)] = total[:, number * ROWS : (number + 1) * ROWS]
 
     side = 1 - 2 * core
     far = (NZ - 2 * side) % NZ
@@ -187,15 +191,14 @@
     for copy in swap:
         copy.wait_recv()
     component_side(1)
+    e_step(0)
     arrival(1, 1)
-    e_step(0)
     arrival(1, 7)
-    arrival(1, 2)
     e_step(1)
-    for rx, rz in ((1, 6), (0, 3), (1, 3)):
+    for rx, rz in ((0, 3), (0, 5), (1, 2), (1, 6)):
         arrival(rx, rz)
     e_step(2)
-    for rx, rz in ((0, 5), (0, 4), (1, 5), (1, 4)):
+    for rx, rz in ((0, 4), (1, 4), (1, 3), (1, 5)):
         arrival(rx, rz)
     e_step(3)
 
@@ -220,12 +223,14 @@
     top = terms[0]
     for term in terms[1:]:
         top = jnp.maximum(top, term)
-    total = jnp.exp(terms[0] - top)
+    total = jnp.exp2(terms[0] - top)
     for term in terms[1:]:
-        total = total + jnp.exp(term - top)
-    norm = top + jnp.log(total)
-    lmax[...] = jnp.exp(lmax[...] - norm)
-    loglik = jnp.sum(jnp.sum(norm, 0, keepdims=True), 1, keepdims=True)
+        total = total + jnp.exp2(term - top)
+    norm = top + jnp.log2(total)
+    for u in range(STEPS):
+        pieces = [norm[rz : rz + 1, ROWS * rx : ROWS * (rx + 1)] for rx, rz in UNITS[u]]
+        scale[pl.ds(u, 1), :] = jnp.exp2(scale[pl.ds(u, 1), :] - jnp.concatenate(pieces, 1))
+    loglik = jnp.sum(jnp.sum(norm, 0, keepdims=True), 1, keepdims=True) * LOG_TWO
     for ref in (cnt, hcnt):
         ref[pl.ds(4, 4), :] = jnp.broadcast_to(loglik, (4, CHUNK))
 
@@ -253,9 +258,8 @@
         acc = jnp.zeros((CHUNK, 2 * D), F32)
         number = jnp.zeros((CHUNK, PAIR), F32)
         comps = pl.ds(COMPS * side + CHUNK * ch, CHUNK)
-        for u, (az, bz) in enumerate(UNITS):
-            scale = jnp.concatenate([lmax[pl.ds(az, 1), :], lmax[pl.ds(bz, 1), :]], 1)
-            r = e_buf[u, comps, :] * scale
+        for u in range(STEPS):
+            r = e_buf[u, comps, :] * scale[pl.ds(u, 1), :]
             number = number + r[:, :PAIR] + r[:, PAIR:]
             hi, lo = split(r)
             acc = acc + dot_nn(hi, f_hi[u]) + dot_nn(lo, f_hi[u]) + dot_nn(hi, f_lo[u])
@@ -385,7 +389,7 @@
             vmem((STEPS, BLOCK, 2 * D), BF16),
             vmem((STEPS, 2 * COMPS, BLOCK), F32),
             vmem((NZ, PAIR), F32),
-            vmem((NZ, PAIR), F32),
+            vmem((8, BLOCK), F32),
             vmem((2 * NZ, NZ, PAIR), F32),
             vmem((CHUNKS, CHUNK, 2 * D), F32),
             vmem((CHUNKS, CHUNK, 2 * D), F32),

time: 50.3 us -> 49.6 us (0.986)
  Pallas kernels: 49.1 us -> 48.3 us
    pallas_call x1, Pallas kernels: 48.5 us -> 47.7 us  [local(): pl.pallas_call(kernel, out_shape=(small,) * 3, in_specs=[pl.BlockSpec(mem...]
where the time goes in v6:
time: 49.6 us; the launch traced here: 49 us
  Pallas kernels  48.3 us (97%)
  between operations  0.64 us (1%)
    pallas_call x1, Pallas kernels, local(): pl.pallas_call(kernel, out_shape=(small,) * 3, in_specs=[pl.BlockSpec(mem...  47.7 us

profile of v6, /device:TPU:1, one launch (start us, length us, event | category | flops | bytes accessed | tf_op | source)
XLA Modules:
  0.0 49.0 jit_solution(17489409480475384427)
XLA Ops:
  0.6 47.7 %em_step.1 = (f32[8,512]{1,0:T(8,128)S(1)}, f32[8,512]{1,0:T(8,128)S(1)}, f32[8,512]{1,0:T(8,128)S(1)}) custom-call(f32[64,128]{1,0:T(8,128)} %x_hbm.1, f32[128,512]{1,0:T(8,128)} %means_hbm.1, f32[128,512]{1,0:T(8,128)} %var_hbm.1, f32[1,512]{1,0:T(1,128)} %bitcast.3), custom_call_target="tpu_custom_call" | custom-call | tf_op jit(solution)/shard_map/em_step/pallas_call | solution.py:375
  48.3 0.6 %write.1 = (f32[8,512]{1,0:T(8,128)}, f32[8,512]{1,0:T(8,128)}, f32[1,512]{1,0:T(1,128)}, f32[1,1]{1,0:T(1,128)}) custom-call(f32[8,512]{1,0:T(8,128)S(1)} %get-tuple-element.11.nm, f32[8,512]{1,0:T(8,128)S(1)} %get-tuple-element.12.nv, f32[8,512]{1,0:T(8,128)S(1)} %get-tuple-element.13.small), custom_call_target="tpu_custom_call" | custom-call | tf_op jit(solution)/shard_map/write/pallas_call | solution.py:435

commit v7 on v6

--- a/solution.py
+++ b/solution.py
@@ -176,6 +176,8 @@
     side = 1 - 2 * core
     far = (NZ - 2 * side) % NZ
     arrival(1, 0)
+    for dz in (1, -1):
+        send(1, 0, dz, 0)
     arrival(0, 6)
     arrival(0, 2)
     send(0, far, 2 * side, 1)
@@ -187,7 +189,6 @@
         send(0, rz, 0, 1)
     for rz in (7, 1):
         arrival(0, rz)
-        send(0, rz, 0, 1)
     for copy in swap:
         copy.wait_recv()
     component_side(1)
@@ -283,37 +284,55 @@
         for dy in FAR_FIRST:
             p2_copy(ch, dy).start()
 
-    for ch in range(CHUNKS):
+    def partner_moments(ch):
         half[ch], number = partial_moments(1, ch)
         hcnt[pl.ds(ch, 1), :] = number
         half_copy(ch).start()
+
+    def own_moments(ch):
+        moments(ch)
+        if ch < LAST:
+            p1_copy(ch).start()
+
     for number in range(2):
         pl.semaphore_wait(hello.at[number], 1)
+    @pl.when(core == 0)
+    def _():
+        for ch in range(CHUNKS):
+            own_moments(ch)
+            partner_moments(ch)
+
+    @pl.when(core == 1)
+    def _():
+        for ch in range(CHUNKS):
+            partner_moments(ch)
+        for ch in range(CHUNKS):
+            own_moments(ch)
+
     hc = remote(hcnt, hcnt_in, hc_s, hc_r, at(0, 0, 1))
     hc.start()
-    for ch in range(LAST):
-        moments(ch)
-        p1_copy(ch).start()
-    moments(LAST)
     for dy in FAR_FIRST:
         p3_copy(dy, 0).start()
     hc.wait_recv()
     cnt[...] = cnt[...] + hcnt_in[...]
-    c1 = remote(cnt, cnt_in, c1_s, c1_r, xlo_peer)
-    c1.start()
+
+    def c1_copy(dy):
+        slot = (NY - dy) % NY
+        return remote(cnt, cnt_in.at[slot], c1_s.at[dy], c1_r.at[slot], y_peer(dy))
+
+    for dy in FAR_FIRST:
+        c1_copy(dy).start()
     pass_on(0)
     pass_on(1)
     for dy in FAR_FIRST + (0,):
         p3_copy(dy, 1).start()
-    c1.wait_recv()
-    cnt2[...] = cnt[...] + cnt_in[...]
-
-    def c2_copy(dy):
-        slot = (NY - dy) % NY
-        return remote(cnt2, cnt2_in.at[slot], c2_s.at[dy], c2_r.at[slot], y_peer(dy))
-
-    for dy in FAR_FIRST:
-        c2_copy(dy).start()
+    totals = cnt[...]
+    for dy in range(1, NY):
+        c1_copy(dy).wait_recv()
+        totals = totals + cnt_in[(NY - dy) % NY]
+    cnt2[...] = totals
+    c2 = remote(cnt2, cnt2_in, c2_s, c2_r, xlo_peer)
+    c2.start()
     pass_on(2)
     others = [(dy, dx) for dy in range(NY) for dx in range(2) if dy or dx]
     sums = [p2[ch, y] for ch in range(LAST)] + [p1[LAST, xlo, y]]
@@ -324,12 +343,10 @@
         for dy in range(1, NY):
             p2_copy(ch, dy).wait_recv()
     for dy in range(1, NY):
-        c2_copy(dy).wait_recv()
-    totals = cnt2[...]
-    for dy in range(1, NY):
-        totals = totals + cnt2_in[dy]
         for ch in range(LAST):
             sums[ch] = sums[ch] + p2_in[ch, dy]
+    c2.wait_recv()
+    totals = totals + cnt2_in[...]
     own = pl.ds(pl.multiple_of(d * 8, 8), 8)
     for ch in range(CHUNKS):
         lanes = pl.ds(ch * CHUNK, CHUNK)
@@ -344,7 +361,7 @@
         loglik = totals[4:5, :] / (TOTAL_ROWS * D)
         small_ref[:, lanes] = jnp.concatenate([log_weights] * 4 + [loglik] * 4, 0)
 
-    for copy in started + swap + [hc, c1]:
+    for copy in started + swap + [hc, c2]:
         copy.wait_send()
     for dz, dx in offsets:
         lse_copy(dz, dx).wait_send()
@@ -357,7 +374,7 @@
     for dy, dx in others:
         p3_copy(dy, dx).wait_send()
     for dy in range(1, NY):
-        c2_copy(dy).wait_send()
+        c1_copy(dy).wait_send()
 
 
 def write(nm, nv, small, nm_out, nv_out, nlw_out, ll_out):
@@ -401,9 +418,9 @@
             vmem((LAST, NY, 16, CHUNK), F32),
             vmem((2 * NY, 16, CHUNK), F32),
             vmem((8, CHUNK), F32),
+            vmem((NY, 8, CHUNK), F32),
             vmem((8, CHUNK), F32),
             vmem((8, CHUNK), F32),
-            vmem((NY, 8, CHUNK), F32),
             pltpu.SemaphoreType.REGULAR((2,)),
             sem((4,)),
             sem((SENDS,)),
@@ -422,10 +439,10 @@
             sem((LAST, NY)),
             sem((2 * NY,)),
             sem((2 * NY,)),
+            sem((NY,)),
+            sem((NY,)),
             sem,
             sem,
-            sem((NY,)),
-            sem((NY,)),
         ],
         compiler_params=pltpu.CompilerParams(
             collective_id=0, has_side_effects=True, vmem_limit_bytes=40 * 2**20

time: 49.6 us -> 50.4 us (1.016)
  Pallas kernels: 48.3 us -> 49.6 us
    pallas_call x1, Pallas kernels: 47.7 us -> 49 us  [local(): pl.pallas_call(kernel, out_shape=(small,) * 3, in_specs=[pl.BlockSpec(mem...]
where the time goes in v7:
time: 50.4 us; the launch traced here: 50.2 us
  Pallas kernels  49.6 us (98%)
  between operations  0.64 us (1%)
    pallas_call x1, Pallas kernels, local(): pl.pallas_call(kernel, out_shape=(small,) * 3, in_specs=[pl.BlockSpec(mem...  49 us

profile of v7, /device:TPU:1, one launch (start us, length us, event | category | flops | bytes accessed | tf_op | source)
XLA Modules:
  0.0 50.2 jit_solution(5537988266354726393)
XLA Ops:
  0.6 49.0 %em_step.1 = (f32[8,512]{1,0:T(8,128)S(1)}, f32[8,512]{1,0:T(8,128)S(1)}, f32[8,512]{1,0:T(8,128)S(1)}) custom-call(f32[64,128]{1,0:T(8,128)} %x_hbm.1, f32[128,512]{1,0:T(8,128)} %means_hbm.1, f32[128,512]{1,0:T(8,128)} %var_hbm.1, f32[1,512]{1,0:T(1,128)} %bitcast.3), custom_call_target="tpu_custom_call" | custom-call | tf_op jit(solution)/shard_map/em_step/pallas_call | solution.py:392
  49.6 0.6 %write.1 = (f32[8,512]{1,0:T(8,128)}, f32[8,512]{1,0:T(8,128)}, f32[1,512]{1,0:T(1,128)}, f32[1,1]{1,0:T(1,128)}) custom-call(f32[8,512]{1,0:T(8,128)S(1)} %get-tuple-element.11.nm, f32[8,512]{1,0:T(8,128)S(1)} %get-tuple-element.12.nv, f32[8,512]{1,0:T(8,128)S(1)} %get-tuple-element.13.small), custom_call_target="tpu_custom_call" | custom-call | tf_op jit(solution)/shard_map/write/pallas_call | solution.py:452

commit v8 on v6

--- a/solution.py
+++ b/solution.py
@@ -97,6 +97,12 @@
             src_ref=src, dst_ref=dst, send_sem=send, recv_sem=recv, device_id=peer, device_id_type=MESH
         )
 
+    def landed(ref, sem):
+        remote(ref, ref, sem, sem, at(0, 0, 1)).wait_recv()
+
+    def left(ref, sem):
+        remote(ref, ref, sem, sem, at(0, 0, 1)).wait_send()
+
     started = []
 
     def held(rx, rz):
@@ -176,6 +182,8 @@
     side = 1 - 2 * core
     far = (NZ - 2 * side) % NZ
     arrival(1, 0)
+    for dz in (1, -1):
+        send(1, 0, dz, 0)
     arrival(0, 6)
     arrival(0, 2)
     send(0, far, 2 * side, 1)
@@ -187,7 +195,6 @@
         send(0, rz, 0, 1)
     for rz in (7, 1):
         arrival(0, rz)
-        send(0, rz, 0, 1)
     for copy in swap:
         copy.wait_recv()
     component_side(1)
@@ -204,13 +211,14 @@
 
     def lse_copy(dz, dx):
         slot = 2 * ((NZ - dz) % NZ) + dx
-        return remote(lse, lse_in.at[slot], l_s.at[2 * dz + dx], l_r.at[slot], at(dz, dx, 0))
+        return remote(lse, lse_in.at[slot], l_s, l_r, at(dz, dx, 0))
 
     offsets = [(dz, dx) for dz in (4, 3, 5, 2, 6, 1, 7, 0) for dx in (1, 0) if (dz, dx) != (0, 0)]
     for dz, dx in offsets:
         lse_copy(dz, dx).start()
-    for dz, dx in offsets:
-        lse_copy(dz, dx).wait_recv()
+    for copy in started + swap:
+        copy.wait_send()
+    landed(lse_in.at[pl.ds(1, 2 * NZ - 1)], l_r)
     terms = [lse[...]]
     for dz, dx in offsets:
         rz = (NZ - dz) % NZ
@@ -240,7 +248,7 @@
     def p2_copy(ch, dy):
         slot = (NY - dy) % NY
         return remote(
-            p2.at[ch, (y + dy) % NY], p2_in.at[ch, slot], p2_s.at[ch, dy], p2_r.at[ch, slot], y_peer(dy)
+            p2.at[ch, (y + dy) % NY], p2_in.at[slot, ch], p2_s, p2_r, y_peer(dy)
         )
 
     def p3_copy(dy, dx):
@@ -248,7 +256,7 @@
         peer_x = 1 - xlo if dx else xlo
         peer_y = (y + dy) % NY
         return remote(
-            p1.at[LAST, peer_x, peer_y], p3_in.at[slot], p3_s.at[2 * dy + dx], p3_r.at[slot], (peer_y * 2 + peer_x, c)
+            p1.at[LAST, peer_x, peer_y], p3_in.at[slot], p3_s, p3_r, (peer_y * 2 + peer_x, c)
         )
 
     def half_copy(ch):
@@ -295,13 +303,17 @@
         moments(ch)
         p1_copy(ch).start()
     moments(LAST)
-    for dy in FAR_FIRST:
-        p3_copy(dy, 0).start()
     hc.wait_recv()
     cnt[...] = cnt[...] + hcnt_in[...]
     c1 = remote(cnt, cnt_in, c1_s, c1_r, xlo_peer)
     c1.start()
+    left(lse_in.at[pl.ds(1, 2 * NZ - 1)], l_s)
+    for ch in range(CHUNKS):
+        half_copy(ch).wait_send()
+    hc.wait_send()
     pass_on(0)
+    for dy in FAR_FIRST:
+        p3_copy(dy, 0).start()
     pass_on(1)
     for dy in FAR_FIRST + (0,):
         p3_copy(dy, 1).start()
@@ -310,26 +322,28 @@
 
     def c2_copy(dy):
         slot = (NY - dy) % NY
-        return remote(cnt2, cnt2_in.at[slot], c2_s.at[dy], c2_r.at[slot], y_peer(dy))
+        return remote(cnt2, cnt2_in.at[slot], c2_s, c2_r, y_peer(dy))
 
     for dy in FAR_FIRST:
         c2_copy(dy).start()
     pass_on(2)
-    others = [(dy, dx) for dy in range(NY) for dx in range(2) if dy or dx]
+    for ch in range(LAST):
+        p1_copy(ch).wait_send()
+    c1.wait_send()
     sums = [p2[ch, y] for ch in range(LAST)] + [p1[LAST, xlo, y]]
-    for dy, dx in others:
-        p3_copy(dy, dx).wait_recv()
-        sums[LAST] = sums[LAST] + p3_in[2 * ((NY - dy) % NY) + dx]
-    for ch in range(LAST):
-        for dy in range(1, NY):
-            p2_copy(ch, dy).wait_recv()
-    for dy in range(1, NY):
-        c2_copy(dy).wait_recv()
+    landed(p3_in.at[pl.ds(1, 2 * NY - 1)], p3_r)
+    for slot in range(1, 2 * NY):
+        sums[LAST] = sums[LAST] + p3_in[slot]
+    landed(cnt2_in.at[pl.ds(1, NY - 1)], c2_r)
     totals = cnt2[...]
-    for dy in range(1, NY):
-        totals = totals + cnt2_in[dy]
+    for slot in range(1, NY):
+        totals = totals + cnt2_in[slot]
+    left(p3_in.at[pl.ds(1, 2 * NY - 1)], p3_s)
+    left(cnt2_in.at[pl.ds(1, NY - 1)], c2_s)
+    landed(p2_in.at[pl.ds(1, NY - 1)], p2_r)
+    for slot in range(1, NY):
         for ch in range(LAST):
-            sums[ch] = sums[ch] + p2_in[ch, dy]
+            sums[ch] = sums[ch] + p2_in[slot, ch]
     own = pl.ds(pl.multiple_of(d * 8, 8), 8)
     for ch in range(CHUNKS):
         lanes = pl.ds(ch * CHUNK, CHUNK)
@@ -344,20 +358,7 @@
         loglik = totals[4:5, :] / (TOTAL_ROWS * D)
         small_ref[:, lanes] = jnp.concatenate([log_weights] * 4 + [loglik] * 4, 0)
 
-    for copy in started + swap + [hc, c1]:
-        copy.wait_send()
-    for dz, dx in offsets:
-        lse_copy(dz, dx).wait_send()
-    for ch in range(CHUNKS):
-        half_copy(ch).wait_send()
-    for ch in range(LAST):
-        p1_copy(ch).wait_send()
-        for dy in range(1, NY):
-            p2_copy(ch, dy).wait_send()
-    for dy, dx in others:
-        p3_copy(dy, dx).wait_send()
-    for dy in range(1, NY):
-        c2_copy(dy).wait_send()
+    left(p2_in.at[pl.ds(1, NY - 1)], p2_s)
 
 
 def write(nm, nv, small, nm_out, nv_out, nlw_out, ll_out):
@@ -398,7 +399,7 @@
             vmem((CHUNKS, 2, NY, 16, CHUNK), F32),
             vmem((LAST, NY, 16, CHUNK), F32),
             vmem((LAST, NY, 16, CHUNK), F32),
-            vmem((LAST, NY, 16, CHUNK), F32),
+            vmem((NY, LAST, 16, CHUNK), F32),
             vmem((2 * NY, 16, CHUNK), F32),
             vmem((8, CHUNK), F32),
             vmem((8, CHUNK), F32),
@@ -410,22 +411,22 @@
             sem((2, NZ)),
             sem((3,)),
             sem((3,)),
-            sem((2 * NZ,)),
-            sem((2 * NZ,)),
+            sem,
+            sem,
             sem((CHUNKS,)),
             sem((CHUNKS,)),
             sem,
             sem,
             sem((LAST,)),
             sem((LAST,)),
-            sem((LAST, NY)),
-            sem((LAST, NY)),
-            sem((2 * NY,)),
-            sem((2 * NY,)),
-            sem,
-            sem,
-            sem((NY,)),
-            sem((NY,)),
+            sem,
+            sem,
+            sem,
+            sem,
+            sem,
+            sem,
+            sem,
+            sem,
         ],
         compiler_params=pltpu.CompilerParams(
             collective_id=0, has_side_effects=True, vmem_limit_bytes=40 * 2**20

time: 49.6 us -> 47.8 us (0.964)
  the two profiles are of different devices: /device:TPU:1 before, /device:TPU:2 now
where the time goes in v8:
time: 47.8 us; the launch traced here: 47.7 us
  Pallas kernels  47.1 us (99%)
  between operations  0.64 us (1%)
    pallas_call x1, Pallas kernels, local(): pl.pallas_call(kernel, out_shape=(small,) * 3, in_specs=[pl.BlockSpec(mem...  46.5 us

profile of v8, /device:TPU:2, one launch (start us, length us, event | category | flops | bytes accessed | tf_op | source)
XLA Modules:
  0.0 47.7 jit_solution(10310970699240048484)
XLA Ops:
  0.6 46.5 %em_step.1 = (f32[8,512]{1,0:T(8,128)S(1)}, f32[8,512]{1,0:T(8,128)S(1)}, f32[8,512]{1,0:T(8,128)S(1)}) custom-call(f32[64,128]{1,0:T(8,128)} %x_hbm.1, f32[128,512]{1,0:T(8,128)} %means_hbm.1, f32[128,512]{1,0:T(8,128)} %var_hbm.1, f32[1,512]{1,0:T(1,128)} %bitcast.3), custom_call_target="tpu_custom_call" | custom-call | tf_op jit(solution)/shard_map/em_step/pallas_call | solution.py:376
  47.1 0.6 %write.1 = (f32[8,512]{1,0:T(8,128)}, f32[8,512]{1,0:T(8,128)}, f32[1,512]{1,0:T(1,128)}, f32[1,1]{1,0:T(1,128)}) custom-call(f32[8,512]{1,0:T(8,128)S(1)} %get-tuple-element.11.nm, f32[8,512]{1,0:T(8,128)S(1)} %get-tuple-element.12.nv, f32[8,512]{1,0:T(8,128)S(1)} %get-tuple-element.13.small), custom_call_target="tpu_custom_call" | custom-call | tf_op jit(solution)/shard_map/write/pallas_call | solution.py:436

commit v9 on v8

--- a/solution.py
+++ b/solution.py
@@ -28,7 +28,8 @@
 FAR_FIRST = (4, 3, 5, 2, 6, 1, 7)
 CHUNK = 128
 CHUNKS = COMPS // CHUNK
-LAST = CHUNKS - 1
+X_FIRST = (2, 3)
+Y_FIRST = (0, 1)
 TOTAL_ROWS = 32768
 TOTAL_COMPS = 16384
 F32, BF16 = jnp.float32, jnp.bfloat16
@@ -51,9 +52,9 @@
     x_hbm, means_hbm, var_hbm, lw_hbm,
     nm_ref, nv_ref, small_ref,
     means, var, lw, xg, p_hi, p_lo, off, f_hi, f_lo, e_buf, lse, scale, lse_in, half, half_in, hcnt, hcnt_in,
-    p1, p1_in, p2, p2_in, p3_in, cnt, cnt_in, cnt2, cnt2_in,
+    p1, p1_in, p2, p2_in, ya, ya_in, yb, yb_in, xs, xs_in, cnt,
     hello, in_sem, g_s, g_r, a_s, a_r, l_s, l_r, h_s, h_r, hc_s, hc_r,
-    p1_s, p1_r, p2_s, p2_r, p3_s, p3_r, c1_s, c1_r, c2_s, c2_r,
+    p1_s, p1_r, p2_s, p2_r, y_s, y_r, x_s, x_r,
 ):
     d = lax.axis_index("dp")
     c = lax.axis_index("comp")
@@ -251,13 +252,10 @@
             p2.at[ch, (y + dy) % NY], p2_in.at[slot, ch], p2_s, p2_r, y_peer(dy)
         )
 
-    def p3_copy(dy, dx):
-        slot = 2 * ((NY - dy) % NY) + dx
-        peer_x = 1 - xlo if dx else xlo
-        peer_y = (y + dy) % NY
-        return remote(
-            p1.at[LAST, peer_x, peer_y], p3_in.at[slot], p3_s, p3_r, (peer_y * 2 + peer_x, c)
-        )
+    def y_copy(j, dy):
+        slot = (NY - dy) % NY
+        src, dst = ((ya, ya_in), (yb, yb_in))[j]
+        return remote(src.at[(y + dy) % NY], dst.at[slot], y_s.at[j], y_r.at[j], y_peer(dy))
 
     def half_copy(ch):
         return remote(half.at[ch], half_in.at[ch], h_s.at[ch], h_r.at[ch], at(0, 0, 1))
@@ -282,8 +280,13 @@
         for side in range(2):
             for ny in range(NY):
                 at_row = 16 * ny + 8 * side
-                p1[ch, side, ny, pl.ds(0, 8), :] = sq[at_row : at_row + 8]
-                p1[ch, side, ny, pl.ds(8, 8), :] = fi[at_row : at_row + 8]
+                if ch in X_FIRST:
+                    p1[X_FIRST.index(ch), side, ny, pl.ds(0, 8), :] = sq[at_row : at_row + 8]
+                    p1[X_FIRST.index(ch), side, ny, pl.ds(8, 8), :] = fi[at_row : at_row + 8]
+                else:
+                    to = (ya, yb)[Y_FIRST.index(ch)]
+                    to[ny, pl.ds(16 * side, 8), :] = sq[at_row : at_row + 8]
+                    to[ny, pl.ds(16 * side + 8, 8), :] = fi[at_row : at_row + 8]
 
     def pass_on(ch):
         p1_copy(ch).wait_recv()
@@ -299,51 +302,54 @@
         pl.semaphore_wait(hello.at[number], 1)
     hc = remote(hcnt, hcnt_in, hc_s, hc_r, at(0, 0, 1))
     hc.start()
-    for ch in range(LAST):
-        moments(ch)
-        p1_copy(ch).start()
-    moments(LAST)
+    moments(0)
+    for dy in FAR_FIRST:
+        y_copy(0, dy).start()
+    moments(1)
+    moments(2)
+    p1_copy(0).start()
+    moments(3)
+    p1_copy(1).start()
     hc.wait_recv()
-    cnt[...] = cnt[...] + hcnt_in[...]
-    c1 = remote(cnt, cnt_in, c1_s, c1_r, xlo_peer)
-    c1.start()
+    for ny in range(NY):
+        yb[ny, pl.ds(32, 8), :] = cnt[...] + hcnt_in[...]
+    for dy in FAR_FIRST:
+        y_copy(1, dy).start()
+    pass_on(0)
+    pass_on(1)
     left(lse_in.at[pl.ds(1, 2 * NZ - 1)], l_s)
     for ch in range(CHUNKS):
         half_copy(ch).wait_send()
     hc.wait_send()
-    pass_on(0)
-    for dy in FAR_FIRST:
-        p3_copy(dy, 0).start()
-    pass_on(1)
-    for dy in FAR_FIRST + (0,):
-        p3_copy(dy, 1).start()
-    c1.wait_recv()
-    cnt2[...] = cnt[...] + cnt_in[...]
-
-    def c2_copy(dy):
-        slot = (NY - dy) % NY
-        return remote(cnt2, cnt2_in.at[slot], c2_s, c2_r, y_peer(dy))
-
-    for dy in FAR_FIRST:
-        c2_copy(dy).start()
-    pass_on(2)
-    for ch in range(LAST):
-        p1_copy(ch).wait_send()
-    c1.wait_send()
-    sums = [p2[ch, y] for ch in range(LAST)] + [p1[LAST, xlo, y]]
-    landed(p3_in.at[pl.ds(1, 2 * NY - 1)], p3_r)
-    for slot in range(1, 2 * NY):
-        sums[LAST] = sums[LAST] + p3_in[slot]
-    landed(cnt2_in.at[pl.ds(1, NY - 1)], c2_r)
-    totals = cnt2[...]
+    for i in range(2):
+        p1_copy(i).wait_send()
+    others = pl.ds(1, NY - 1)
+    landed(ya_in.at[others], y_r.at[0])
+    total_a = ya[y]
     for slot in range(1, NY):
-        totals = totals + cnt2_in[slot]
-    left(p3_in.at[pl.ds(1, 2 * NY - 1)], p3_s)
-    left(cnt2_in.at[pl.ds(1, NY - 1)], c2_s)
-    landed(p2_in.at[pl.ds(1, NY - 1)], p2_r)
+        total_a = total_a + ya_in[slot]
+    landed(yb_in.at[others], y_r.at[1])
+    total_b = yb[y]
     for slot in range(1, NY):
-        for ch in range(LAST):
-            sums[ch] = sums[ch] + p2_in[slot, ch]
+        total_b = total_b + yb_in[slot]
+    for side in range(2):
+        xs[side, pl.ds(0, 16), :] = total_a[16 * side : 16 * side + 16]
+        xs[side, pl.ds(16, 16), :] = total_b[16 * side : 16 * side + 16]
+        xs[side, pl.ds(32, 8), :] = total_b[32:]
+    x_copy = remote(xs.at[1 - xlo], xs_in, x_s, x_r, xlo_peer)
+    x_copy.start()
+    left(ya_in.at[others], y_s.at[0])
+    left(yb_in.at[others], y_s.at[1])
+    landed(p2_in.at[others], p2_r)
+    sums = [p2[i, y] for i in range(2)]
+    for slot in range(1, NY):
+        for i in range(2):
+            sums[i] = sums[i] + p2_in[slot, i]
+    left(p2_in.at[others], p2_s)
+    x_copy.wait()
+    last = xs[xlo] + xs_in[...]
+    totals = last[32:]
+    sums = [last[:16], last[16:32], sums[0], sums[1]]
     own = pl.ds(pl.multiple_of(d * 8, 8), 8)
     for ch in range(CHUNKS):
         lanes = pl.ds(ch * CHUNK, CHUNK)
@@ -357,8 +363,6 @@
         log_weights = jnp.log(denom / (TOTAL_ROWS + TOTAL_COMPS * PRIOR))
         loglik = totals[4:5, :] / (TOTAL_ROWS * D)
         small_ref[:, lanes] = jnp.concatenate([log_weights] * 4 + [loglik] * 4, 0)
-
-    left(p2_in.at[pl.ds(1, NY - 1)], p2_s)
 
 
 def write(nm, nv, small, nm_out, nv_out, nlw_out, ll_out):
@@ -396,15 +400,17 @@
             vmem((CHUNKS, CHUNK, 2 * D), F32),
             vmem((8, CHUNK), F32),
             vmem((8, CHUNK), F32),
-            vmem((CHUNKS, 2, NY, 16, CHUNK), F32),
-            vmem((LAST, NY, 16, CHUNK), F32),
-            vmem((LAST, NY, 16, CHUNK), F32),
-            vmem((NY, LAST, 16, CHUNK), F32),
-            vmem((2 * NY, 16, CHUNK), F32),
+            vmem((2, 2, NY, 16, CHUNK), F32),
+            vmem((2, NY, 16, CHUNK), F32),
+            vmem((2, NY, 16, CHUNK), F32),
+            vmem((NY, 2, 16, CHUNK), F32),
+            vmem((NY, 32, CHUNK), F32),
+            vmem((NY, 32, CHUNK), F32),
+            vmem((NY, 40, CHUNK), F32),
+            vmem((NY, 40, CHUNK), F32),
+            vmem((2, 40, CHUNK), F32),
+            vmem((40, CHUNK), F32),
             vmem((8, CHUNK), F32),
-            vmem((8, CHUNK), F32),
-            vmem((8, CHUNK), F32),
-            vmem((NY, 8, CHUNK), F32),
             pltpu.SemaphoreType.REGULAR((2,)),
             sem((4,)),
             sem((SENDS,)),
@@ -417,14 +423,12 @@
             sem((CHUNKS,)),
             sem,
             sem,
-            sem((LAST,)),
-            sem((LAST,)),
-            sem,
-            sem,
-            sem,
-            sem,
-            sem,
-            sem,
+            sem((2,)),
+            sem((2,)),
+            sem,
+            sem,
+            sem((2,)),
+            sem((2,)),
             sem,
             sem,
         ],

time: 47.8 us -> 47.3 us (0.990)
  the two profiles are of different devices: /device:TPU:2 before, /device:TPU:1 now
where the time goes in v9:
time: 47.3 us; the launch traced here: 47.2 us
  Pallas kernels  46.5 us (98%)
  between operations  0.64 us (1%)
    pallas_call x1, Pallas kernels, local(): pl.pallas_call(kernel, out_shape=(small,) * 3, in_specs=[pl.BlockSpec(mem...  45.9 us

profile of v9, /device:TPU:1, one launch (start us, length us, event | category | flops | bytes accessed | tf_op | source)
XLA Modules:
  0.0 47.2 jit_solution(11429198450045061378)
XLA Ops:
  0.6 45.9 %em_step.1 = (f32[8,512]{1,0:T(8,128)S(1)}, f32[8,512]{1,0:T(8,128)S(1)}, f32[8,512]{1,0:T(8,128)S(1)}) custom-call(f32[64,128]{1,0:T(8,128)} %x_hbm.1, f32[128,512]{1,0:T(8,128)} %means_hbm.1, f32[128,512]{1,0:T(8,128)} %var_hbm.1, f32[1,512]{1,0:T(1,128)} %bitcast.3), custom_call_target="tpu_custom_call" | custom-call | tf_op jit(solution)/shard_map/em_step/pallas_call | solution.py:380
  46.6 0.6 %write.1 = (f32[8,512]{1,0:T(8,128)}, f32[8,512]{1,0:T(8,128)}, f32[1,512]{1,0:T(1,128)}, f32[1,1]{1,0:T(1,128)}) custom-call(f32[8,512]{1,0:T(8,128)S(1)} %get-tuple-element.11.nm, f32[8,512]{1,0:T(8,128)S(1)} %get-tuple-element.12.nv, f32[8,512]{1,0:T(8,128)S(1)} %get-tuple-element.13.small), custom_call_target="tpu_custom_call" | custom-call | tf_op jit(solution)/shard_map/write/pallas_call | solution.py:440

commit v10 on v8

--- a/solution.py
+++ b/solution.py
@@ -28,7 +28,7 @@
 FAR_FIRST = (4, 3, 5, 2, 6, 1, 7)
 CHUNK = 128
 CHUNKS = COMPS // CHUNK
-LAST = CHUNKS - 1
+Y_CHUNKS = 2
 TOTAL_ROWS = 32768
 TOTAL_COMPS = 16384
 F32, BF16 = jnp.float32, jnp.bfloat16
@@ -51,9 +51,9 @@
     x_hbm, means_hbm, var_hbm, lw_hbm,
     nm_ref, nv_ref, small_ref,
     means, var, lw, xg, p_hi, p_lo, off, f_hi, f_lo, e_buf, lse, scale, lse_in, half, half_in, hcnt, hcnt_in,
-    p1, p1_in, p2, p2_in, p3_in, cnt, cnt_in, cnt2, cnt2_in,
+    p1, p1_in, p2, p2_in, y_in, xs, xs_in, fin, cnt, cnt_in, cnt2, cnt2_in,
     hello, in_sem, g_s, g_r, a_s, a_r, l_s, l_r, h_s, h_r, hc_s, hc_r,
-    p1_s, p1_r, p2_s, p2_r, p3_s, p3_r, c1_s, c1_r, c2_s, c2_r,
+    p1_s, p1_r, p2_s, p2_r, y_s, y_r, x_s, x_r, c1_s, c1_r, c2_s, c2_r,
 ):
     d = lax.axis_index("dp")
     c = lax.axis_index("comp")
@@ -73,6 +73,11 @@
 
     xlo_peer = (y * 2 + 1 - xlo, c)
 
+    barrier = pltpu.get_barrier_semaphore()
+    peers = [at(dz, 0, 0) for dz in (1, 7, 2, 6)] + [at(0, 1, 0), at(0, 0, 1), xlo_peer]
+    peers += [y_peer(dy) for dy in (1, 7, 2, 6)]
+    for peer in peers:
+        pl.semaphore_signal(barrier, inc=1, device_id=peer, device_id_type=MESH)
     local_in = [
         pltpu.make_async_copy(means_hbm, means.at[0], in_sem.at[0]),
         pltpu.make_async_copy(var_hbm, var.at[0], in_sem.at[1]),
@@ -81,12 +86,6 @@
     ]
     for copy in local_in:
         copy.start()
-
-    barrier = pltpu.get_barrier_semaphore()
-    peers = [at(dz, 0, 0) for dz in (1, 7, 2, 6)] + [at(0, 1, 0), at(0, 0, 1), xlo_peer]
-    peers += [y_peer(dy) for dy in (1, 7, 2, 6)]
-    for peer in peers:
-        pl.semaphore_signal(barrier, inc=1, device_id=peer, device_id_type=MESH)
     pl.semaphore_wait(barrier, len(peers))
 
     def block(rx, rz):
@@ -251,13 +250,13 @@
             p2.at[ch, (y + dy) % NY], p2_in.at[slot, ch], p2_s, p2_r, y_peer(dy)
         )
 
-    def p3_copy(dy, dx):
-        slot = 2 * ((NY - dy) % NY) + dx
-        peer_x = 1 - xlo if dx else xlo
-        peer_y = (y + dy) % NY
-        return remote(
-            p1.at[LAST, peer_x, peer_y], p3_in.at[slot], p3_s, p3_r, (peer_y * 2 + peer_x, c)
-        )
+    def y_copy(ch, dy):
+        slot = (NY - dy) % NY
+        return remote(p1.at[ch, :, (y + dy) % NY], y_in.at[slot, ch], y_s, y_r, y_peer(dy))
+
+    def count_copy(src, dy):
+        slot = (NY - dy) % NY
+        return remote(src, cnt2_in.at[slot], c2_s, c2_r, y_peer(dy))
 
     def half_copy(ch):
         return remote(half.at[ch], half_in.at[ch], h_s.at[ch], h_r.at[ch], at(0, 0, 1))
@@ -299,51 +298,99 @@
         pl.semaphore_wait(hello.at[number], 1)
     hc = remote(hcnt, hcnt_in, hc_s, hc_r, at(0, 0, 1))
     hc.start()
-    for ch in range(LAST):
+    for ch in range(CHUNKS):
         moments(ch)
-        p1_copy(ch).start()
-    moments(LAST)
+
+        @pl.when(core == 0)
+        def _():
+            p1_copy(ch).start()
+
+        @pl.when(core == 1)
+        def _():
+            if ch < Y_CHUNKS:
+                for dy in FAR_FIRST:
+                    y_copy(ch, dy).start()
+            else:
+                p1_copy(ch).start()
+
     hc.wait_recv()
     cnt[...] = cnt[...] + hcnt_in[...]
-    c1 = remote(cnt, cnt_in, c1_s, c1_r, xlo_peer)
-    c1.start()
-    left(lse_in.at[pl.ds(1, 2 * NZ - 1)], l_s)
-    for ch in range(CHUNKS):
-        half_copy(ch).wait_send()
-    hc.wait_send()
-    pass_on(0)
-    for dy in FAR_FIRST:
-        p3_copy(dy, 0).start()
-    pass_on(1)
-    for dy in FAR_FIRST + (0,):
-        p3_copy(dy, 1).start()
-    c1.wait_recv()
-    cnt2[...] = cnt[...] + cnt_in[...]
-
-    def c2_copy(dy):
-        slot = (NY - dy) % NY
-        return remote(cnt2, cnt2_in.at[slot], c2_s, c2_r, y_peer(dy))
-
-    for dy in FAR_FIRST:
-        c2_copy(dy).start()
-    pass_on(2)
-    for ch in range(LAST):
-        p1_copy(ch).wait_send()
-    c1.wait_send()
-    sums = [p2[ch, y] for ch in range(LAST)] + [p1[LAST, xlo, y]]
-    landed(p3_in.at[pl.ds(1, 2 * NY - 1)], p3_r)
-    for slot in range(1, 2 * NY):
-        sums[LAST] = sums[LAST] + p3_in[slot]
-    landed(cnt2_in.at[pl.ds(1, NY - 1)], c2_r)
-    totals = cnt2[...]
-    for slot in range(1, NY):
-        totals = totals + cnt2_in[slot]
-    left(p3_in.at[pl.ds(1, 2 * NY - 1)], p3_s)
-    left(cnt2_in.at[pl.ds(1, NY - 1)], c2_s)
-    landed(p2_in.at[pl.ds(1, NY - 1)], p2_r)
-    for slot in range(1, NY):
-        for ch in range(LAST):
-            sums[ch] = sums[ch] + p2_in[slot, ch]
+    others = pl.ds(1, NY - 1)
+    counts_at = pl.ds(16 * CHUNKS, 8)
+
+    def sent_before():
+        left(lse_in.at[pl.ds(1, 2 * NZ - 1)], l_s)
+        for ch in range(CHUNKS):
+            half_copy(ch).wait_send()
+        hc.wait_send()
+
+    @pl.when(core == 0)
+    def _():
+        c1 = remote(cnt, cnt_in, c1_s, c1_r, xlo_peer)
+        c1.start()
+        sent_before()
+        for ch in range(CHUNKS):
+            pass_on(ch)
+        c1.wait()
+        cnt2[...] = cnt[...] + cnt_in[...]
+        for dy in FAR_FIRST:
+            count_copy(cnt2, dy).start()
+        for ch in range(CHUNKS):
+            p1_copy(ch).wait_send()
+        landed(p2_in.at[others], p2_r)
+        for ch in range(CHUNKS):
+            total = p2[ch, y]
+            for slot in range(1, NY):
+                total = total + p2_in[slot, ch]
+            fin[pl.ds(16 * ch, 16), :] = total
+        landed(cnt2_in.at[others], c2_r)
+        total = cnt2[...]
+        for slot in range(1, NY):
+            total = total + cnt2_in[slot]
+        fin[counts_at, :] = total
+        left(p2_in.at[others], p2_s)
+        left(cnt2_in.at[others], c2_s)
+
+    @pl.when(core == 1)
+    def _():
+        for dy in FAR_FIRST:
+            count_copy(cnt, dy).start()
+        sent_before()
+        for ch in range(Y_CHUNKS, CHUNKS):
+            pass_on(ch)
+        landed(y_in.at[others], y_r)
+        for ch in range(Y_CHUNKS):
+            for side in range(2):
+                total = p1[ch, side, y]
+                for slot in range(1, NY):
+                    total = total + y_in[slot, ch, side]
+                xs[side, pl.ds(16 * ch, 16), :] = total
+        landed(cnt2_in.at[others], c2_r)
+        total = cnt[...]
+        for slot in range(1, NY):
+            total = total + cnt2_in[slot]
+        for side in range(2):
+            xs[side, pl.ds(16 * Y_CHUNKS, 8), :] = total
+        x_copy = remote(xs.at[1 - xlo], xs_in, x_s, x_r, xlo_peer)
+        x_copy.start()
+        left(y_in.at[others], y_s)
+        left(cnt2_in.at[others], c2_s)
+        rest = pl.ds(Y_CHUNKS, CHUNKS - Y_CHUNKS)
+        landed(p2_in.at[others, rest], p2_r)
+        for ch in range(Y_CHUNKS, CHUNKS):
+            p1_copy(ch).wait_send()
+            total = p2[ch, y]
+            for slot in range(1, NY):
+                total = total + p2_in[slot, ch]
+            fin[pl.ds(16 * ch, 16), :] = total
+        left(p2_in.at[others, rest], p2_s)
+        x_copy.wait()
+        total = xs[xlo] + xs_in[...]
+        fin[pl.ds(0, 16 * Y_CHUNKS), :] = total[: 16 * Y_CHUNKS]
+        fin[counts_at, :] = total[16 * Y_CHUNKS :]
+
+    totals = fin[counts_at, :]
+    sums = [fin[pl.ds(16 * ch, 16), :] for ch in range(CHUNKS)]
     own = pl.ds(pl.multiple_of(d * 8, 8), 8)
     for ch in range(CHUNKS):
         lanes = pl.ds(ch * CHUNK, CHUNK)
@@ -357,8 +404,6 @@
         log_weights = jnp.log(denom / (TOTAL_ROWS + TOTAL_COMPS * PRIOR))
         loglik = totals[4:5, :] / (TOTAL_ROWS * D)
         small_ref[:, lanes] = jnp.concatenate([log_weights] * 4 + [loglik] * 4, 0)
-
-    left(p2_in.at[pl.ds(1, NY - 1)], p2_s)
 
 
 def write(nm, nv, small, nm_out, nv_out, nlw_out, ll_out):
@@ -397,10 +442,13 @@
             vmem((8, CHUNK), F32),
             vmem((8, CHUNK), F32),
             vmem((CHUNKS, 2, NY, 16, CHUNK), F32),
-            vmem((LAST, NY, 16, CHUNK), F32),
-            vmem((LAST, NY, 16, CHUNK), F32),
-            vmem((NY, LAST, 16, CHUNK), F32),
-            vmem((2 * NY, 16, CHUNK), F32),
+            vmem((CHUNKS, NY, 16, CHUNK), F32),
+            vmem((CHUNKS, NY, 16, CHUNK), F32),
+            vmem((NY, CHUNKS, 16, CHUNK), F32),
+            vmem((NY, Y_CHUNKS, 2, 16, CHUNK), F32),
+            vmem((2, 16 * Y_CHUNKS + 8, CHUNK), F32),
+            vmem((16 * Y_CHUNKS + 8, CHUNK), F32),
+            vmem((16 * CHUNKS + 8, CHUNK), F32),
             vmem((8, CHUNK), F32),
             vmem((8, CHUNK), F32),
             vmem((8, CHUNK), F32),
@@ -417,8 +465,10 @@
             sem((CHUNKS,)),
             sem,
             sem,
-            sem((LAST,)),
-            sem((LAST,)),
+            sem((CHUNKS,)),
+            sem((CHUNKS,)),
+            sem,
+            sem,
             sem,
             sem,
             sem,

time: 47.8 us -> 47.7 us (level)
  no operation moved by 1% of the time
where the time goes in v10:
time: 47.7 us; the launch traced here: 47.6 us
  Pallas kernels  46.9 us (98%)
  between operations  0.64 us (1%)
    pallas_call x1, Pallas kernels, local(): pl.pallas_call(kernel, out_shape=(small,) * 3, in_specs=[pl.BlockSpec(mem...  46.3 us

profile of v10, /device:TPU:2, one launch (start us, length us, event | category | flops | bytes accessed | tf_op | source)
XLA Modules:
  0.0 47.6 jit_solution(12868749223588847388)
XLA Ops:
  0.6 46.3 %em_step.1 = (f32[8,512]{1,0:T(8,128)S(1)}, f32[8,512]{1,0:T(8,128)S(1)}, f32[8,512]{1,0:T(8,128)S(1)}) custom-call(f32[64,128]{1,0:T(8,128)} %x_hbm.1, f32[128,512]{1,0:T(8,128)} %means_hbm.1, f32[128,512]{1,0:T(8,128)} %var_hbm.1, f32[1,512]{1,0:T(1,128)} %bitcast.3), custom_call_target="tpu_custom_call" | custom-call | tf_op jit(solution)/shard_map/em_step/pallas_call | solution.py:421
  46.9 0.6 %write.1 = (f32[8,512]{1,0:T(8,128)}, f32[8,512]{1,0:T(8,128)}, f32[1,512]{1,0:T(1,128)}, f32[1,1]{1,0:T(1,128)}) custom-call(f32[8,512]{1,0:T(8,128)S(1)} %get-tuple-element.11.nm, f32[8,512]{1,0:T(8,128)S(1)} %get-tuple-element.12.nv, f32[8,512]{1,0:T(8,128)S(1)} %get-tuple-element.13.small), custom_call_target="tpu_custom_call" | custom-call | tf_op jit(solution)/shard_map/write/pallas_call | solution.py:486

commit v11 on v10

--- a/solution.py
+++ b/solution.py
@@ -28,7 +28,7 @@
 FAR_FIRST = (4, 3, 5, 2, 6, 1, 7)
 CHUNK = 128
 CHUNKS = COMPS // CHUNK
-Y_CHUNKS = 2
+Y_CHUNKS = 3
 TOTAL_ROWS = 32768
 TOTAL_COMPS = 16384
 F32, BF16 = jnp.float32, jnp.bfloat16

time: 47.7 us -> 47.1 us (0.987)
  Pallas kernels: 46.9 us -> 46.3 us
    pallas_call x1, Pallas kernels: 46.3 us -> 45.7 us  [local(): pl.pallas_call(kernel, out_shape=(small,) * 3, in_specs=[pl.BlockSpec(mem...]
where the time goes in v11:
time: 47.1 us; the launch traced here: 47 us
  Pallas kernels  46.3 us (98%)
  between operations  0.64 us (1%)
    pallas_call x1, Pallas kernels, local(): pl.pallas_call(kernel, out_shape=(small,) * 3, in_specs=[pl.BlockSpec(mem...  45.7 us

profile of v11, /device:TPU:2, one launch (start us, length us, event | category | flops | bytes accessed | tf_op | source)
XLA Modules:
  0.0 47.0 jit_solution(14551814267502996926)
XLA Ops:
  0.6 45.7 %em_step.1 = (f32[8,512]{1,0:T(8,128)S(1)}, f32[8,512]{1,0:T(8,128)S(1)}, f32[8,512]{1,0:T(8,128)S(1)}) custom-call(f32[64,128]{1,0:T(8,128)} %x_hbm.1, f32[128,512]{1,0:T(8,128)} %means_hbm.1, f32[128,512]{1,0:T(8,128)} %var_hbm.1, f32[1,512]{1,0:T(1,128)} %bitcast.3), custom_call_target="tpu_custom_call" | custom-call | tf_op jit(solution)/shard_map/em_step/pallas_call | solution.py:421
  46.4 0.6 %write.1 = (f32[8,512]{1,0:T(8,128)}, f32[8,512]{1,0:T(8,128)}, f32[1,512]{1,0:T(1,128)}, f32[1,1]{1,0:T(1,128)}) custom-call(f32[8,512]{1,0:T(8,128)S(1)} %get-tuple-element.11.nm, f32[8,512]{1,0:T(8,128)S(1)} %get-tuple-element.12.nv, f32[8,512]{1,0:T(8,128)S(1)} %get-tuple-element.13.small), custom_call_target="tpu_custom_call" | custom-call | tf_op jit(solution)/shard_map/write/pallas_call | solution.py:486

commit v12 on v11

--- a/solution.py
+++ b/solution.py
@@ -326,15 +326,18 @@
 
     @pl.when(core == 0)
     def _():
-        c1 = remote(cnt, cnt_in, c1_s, c1_r, xlo_peer)
-        c1.start()
+        for dy in FAR_FIRST:
+            count_copy(cnt, dy).start()
         sent_before()
         for ch in range(CHUNKS):
             pass_on(ch)
-        c1.wait()
-        cnt2[...] = cnt[...] + cnt_in[...]
-        for dy in FAR_FIRST:
-            count_copy(cnt2, dy).start()
+        landed(cnt2_in.at[others], c2_r)
+        total = cnt[...]
+        for slot in range(1, NY):
+            total = total + cnt2_in[slot]
+        cnt2[...] = total
+        c1 = remote(cnt2, cnt_in, c1_s, c1_r, xlo_peer)
+        c1.start()
         for ch in range(CHUNKS):
             p1_copy(ch).wait_send()
         landed(p2_in.at[others], p2_r)
@@ -343,11 +346,8 @@
             for slot in range(1, NY):
                 total = total + p2_in[slot, ch]
             fin[pl.ds(16 * ch, 16), :] = total
-        landed(cnt2_in.at[others], c2_r)
-        total = cnt2[...]
-        for slot in range(1, NY):
-            total = total + cnt2_in[slot]
-        fin[counts_at, :] = total
+        c1.wait()
+        fin[counts_at, :] = cnt2[...] + cnt_in[...]
         left(p2_in.at[others], p2_s)
         left(cnt2_in.at[others], c2_s)
 

time: 47.1 us -> 46.5 us (0.987)
  the two profiles are of different devices: /device:TPU:2 before, /device:TPU:1 now
where the time goes in v12:
time: 46.5 us; the launch traced here: 46.1 us
  Pallas kernels  45.5 us (98%)
  between operations  0.64 us (1%)
    pallas_call x1, Pallas kernels, local(): pl.pallas_call(kernel, out_shape=(small,) * 3, in_specs=[pl.BlockSpec(mem...  44.9 us

profile of v12, /device:TPU:1, one launch (start us, length us, event | category | flops | bytes accessed | tf_op | source)
XLA Modules:
  0.0 46.1 jit_solution(10653290243827352516)
XLA Ops:
  0.6 44.9 %em_step.1 = (f32[8,512]{1,0:T(8,128)S(1)}, f32[8,512]{1,0:T(8,128)S(1)}, f32[8,512]{1,0:T(8,128)S(1)}) custom-call(f32[64,128]{1,0:T(8,128)} %x_hbm.1, f32[128,512]{1,0:T(8,128)} %means_hbm.1, f32[128,512]{1,0:T(8,128)} %var_hbm.1, f32[1,512]{1,0:T(1,128)} %bitcast.3), custom_call_target="tpu_custom_call" | custom-call | tf_op jit(solution)/shard_map/em_step/pallas_call | solution.py:421
  45.5 0.6 %write.1 = (f32[8,512]{1,0:T(8,128)}, f32[8,512]{1,0:T(8,128)}, f32[1,512]{1,0:T(1,128)}, f32[1,1]{1,0:T(1,128)}) custom-call(f32[8,512]{1,0:T(8,128)S(1)} %get-tuple-element.11.nm, f32[8,512]{1,0:T(8,128)S(1)} %get-tuple-element.12.nv, f32[8,512]{1,0:T(8,128)S(1)} %get-tuple-element.13.small), custom_call_target="tpu_custom_call" | custom-call | tf_op jit(solution)/shard_map/write/pallas_call | solution.py:486
